TPU v7x, 512 devices: a whole 4x8x8 slice. The times are simulated.
512 devices in a mesh: blk: 64 (over z_lo, y, core), txt: 8 (over z_hi, x).
Axes of the slice: x: 4, y: 8, z: 8 (z_hi: 2, z_lo: 4; z = z_hi * 4 + z_lo), core: 2. Of those that a mesh axis runs over, the one named last changes fastest.
Arguments:
- image_student: bfloat16 [8192, 768], P('blk'), may hold values from -40 to 40
- head_weight: bfloat16 [768, 768], replicated, may hold values from -0.21875 to 0.21875
- text_student: bfloat16 [8192, 768], P(('blk', 'txt')), may hold values from -0.8 to 0.8
- image_teacher: bfloat16 [8192, 1152], P('blk'), may hold values from -40 to 40
- text_teacher: bfloat16 [8192, 1152], P(('blk', 'txt')), may hold values from -40 to 40
- logit_scales: float32 [2], replicated, may hold values from 5 to 15
- logit_biases: float32 [2], replicated, may hold values from -4 to -1
- loss_scale: float32 [1], replicated, may hold values from 256 to 1024
Outputs:
- head_grad: float32 [768, 768], P('blk')
- text_grad: float32 [8192, 768], P(('blk', 'txt'))
- row_loss: float32 [8192], P('blk')
All inputs are finite; a program needn't handle non-finite values.
Results may differ from a plain program's by a relative error of at most 0.0039.
Values may be sent and summed in bfloat16 or wider, within the bound.
A program may use at most 64 MiB of HBM per device.

v0:
```python
import jax
import jax.numpy as jnp
from jax import lax
from jax.sharding import PartitionSpec as P

epsilon = 1e-06


def shifted(value, axis, steps):
    count = lax.axis_size(axis)
    pairs = [(source, (source + steps) % count) for source in range(count)]
    return lax.ppermute(value, axis, pairs)


def normalize(matrix):
    widened = matrix.astype(jnp.float32)
    radius = jnp.sqrt(jnp.sum(widened * widened, axis=1, keepdims=True) + epsilon)
    return (widened / radius, radius)


def pull_back(grad_unit, unit_rows, radius):
    radial = jnp.sum(grad_unit * unit_rows, axis=1, keepdims=True)
    return (grad_unit - unit_rows * radial) / radius


def contract_last(first_operand, second_operand):
    return lax.dot_general(
        first_operand, second_operand, (((1,), (1,)), ((), ())), preferred_element_type=jnp.float32
    )


def shards(
    image_student,
    head_weight,
    text_student,
    image_teacher,
    text_teacher,
    logit_scales,
    logit_biases,
    loss_scale,
):
    block_count = lax.axis_size("blk")
    img_count = image_student.shape[0]
    txt_count = text_student.shape[0]
    width = head_weight.shape[1]
    batch_total = img_count * block_count
    projected = jnp.dot(image_student, head_weight, preferred_element_type=jnp.float32)
    image_unit, image_radius = normalize(projected)
    image_low = image_unit.astype(jnp.bfloat16)
    text_unit, text_radius = normalize(text_student)
    text_low = text_unit.astype(jnp.bfloat16)
    teach_image = normalize(image_teacher)[0].astype(jnp.bfloat16)
    teach_text = normalize(text_teacher)[0].astype(jnp.bfloat16)
    factor = loss_scale[0] * logit_scales[0] / batch_total

    def pair_tile(text_rows, teach_rows):
        student = logit_scales[0] * contract_last(text_rows, image_low) + logit_biases[0]
        teacher = logit_scales[1] * contract_last(teach_rows, teach_image) + logit_biases[1]
        target = jax.nn.sigmoid(teacher)
        pair_loss = jax.nn.softplus(student) - target * student
        errors = (jax.nn.sigmoid(student) - target).astype(jnp.bfloat16)
        text_term = factor * jnp.dot(errors, image_low, preferred_element_type=jnp.float32)
        return (jnp.sum(pair_loss, axis=0), errors, text_term)

    def record(stores, turn_index, errors, text_rows):
        err_store, text_store = stores
        store_offset = (turn_index * txt_count).astype(jnp.int32)
        zero_index = jnp.zeros((), jnp.int32)
        err_store = lax.dynamic_update_slice(err_store, errors, (store_offset, zero_index))
        text_store = lax.dynamic_update_slice(text_store, text_rows, (store_offset, zero_index))
        return (err_store, text_store)

    stores = (
        jnp.zeros((block_count * txt_count, img_count), jnp.bfloat16),
        jnp.zeros((block_count * txt_count, width), jnp.bfloat16),
    )
    loss_rows = jnp.zeros((img_count,), jnp.float32)

    def advance(turn_index, state_now):
        text_rows, teach_rows, grad_rows, loss_rows, stores = state_now
        row_part, errors, text_term = pair_tile(text_rows, teach_rows)
        stores = record(stores, turn_index, errors, text_rows)
        text_rows, teach_rows = shifted((text_rows, teach_rows), "blk", 1)
        grad_rows = shifted(grad_rows + text_term, "blk", 1)
        return (text_rows, teach_rows, grad_rows, loss_rows + row_part, stores)

    start_state = (
        text_low,
        teach_text,
        jnp.zeros((txt_count, width), jnp.float32),
        loss_rows,
        stores,
    )
    final_state = lax.fori_loop(0, block_count, advance, start_state)
    text_acc = final_state[2]
    loss_rows = final_state[3]
    stores = final_state[4]
    err_store, text_store = stores
    image_grad = factor * lax.dot_general(
        err_store, text_store, (((0,), (0,)), ((), ())), preferred_element_type=jnp.float32
    )
    image_wide = image_student.astype(jnp.float32)
    image_step = pull_back(image_grad, image_unit, image_radius)
    head_rows = lax.psum_scatter(
        jnp.dot(image_wide.T, image_step, precision=lax.Precision.HIGHEST),
        "blk",
        scatter_dimension=0,
        tiled=True,
    )
    head_rows, loss_rows = lax.psum((head_rows, loss_rows), "txt")
    text_grad = pull_back(text_acc, text_unit, text_radius)
    return (head_rows, text_grad, loss_rows / batch_total)


def solution(mesh):
    placed = (
        P("blk", None),
        P(),
        P(("blk", "txt"), None),
        P("blk", None),
        P(("blk", "txt"), None),
        P(),
        P(),
        P(),
    )
    return jax.shard_map(
        shards,
        mesh=mesh,
        in_specs=placed,
        out_specs=(P("blk", None), P(("blk", "txt"), None), P("blk")),
        check_vma=False,
    )
```

profile of v0, /device:TPU:1, one launch (start us, length us, event | category | flops | bytes accessed | tf_op | source)
XLA Modules:
  0.0 1698.7 jit_solution(6731312939138052134)
XLA Ops:
  12.7 1084.7 %while.24 = (s32[]{:T(128)}, bf16[16,768]{1,0:T(8,128)(2,1)S(1)}, bf16[16,1152]{1,0:T(8,128)(2,1)S(1)}, f32[16,768]{1,0:T(8,128)S(1)}, f32[128]{0:T(128)S(1)}, /...) while((s32[]{:T(128)}, bf16[16,768]{1,0:T(8,128)(2,1)S(1)}, ...), condition=%wide.region_6.7_spmd.clone, body=%wide.region_4.6_spmd.clone.sunk | while | flops 11077767 | bytes 1517953 | solution.py:94
  58.1 5.7 collective-permute-done.2
  108.9 5.7 collective-permute-done.2
  125.8 5.7 collective-permute-done.2
  142.8 5.7 collective-permute-done.2
  159.7 5.7 collective-permute-done.2
  227.5 5.7 collective-permute-done.2
  244.4 5.7 collective-permute-done.2
  261.4 5.7 collective-permute-done.2
  329.2 5.7 collective-permute-done.2
  346.1 5.7 collective-permute-done.2
  363.1 5.7 collective-permute-done.2
  380.0 5.7 collective-permute-done.2
  430.8 5.7 collective-permute-done.2
  447.8 5.7 collective-permute-done.2
  464.7 5.7 collective-permute-done.2
  481.7 5.7 collective-permute-done.2
  549.5 5.7 collective-permute-done.2
  566.4 5.7 collective-permute-done.2
  583.4 5.7 collective-permute-done.2
  651.1 5.7 collective-permute-done.2
  668.1 5.7 collective-permute-done.2
  1104.8 533.2 %all-reduce.4.cloned.1.call-done = f32[768,768]{0,1:T(8,128)} async-done(((f32[768,768]{0,1:T(8,128)}), f32[768,768]{0,1:T(8,128)}) %all-reduce.4.cloned.1.call-update) | async-done | bytes 2359312
  1639.4 51.2 %all-reduce.1 = (f32[12,768]{0,1:T(8,128)S(1)}, f32[128]{0:T(128)S(1)}) all-reduce(f32[12,768]{0,1:T(8,128)S(1)} %constant_dynamic-slice_fusion, f32[128]{0:T(128)S(1)} %get-tuple-element.208), channel_id=1, replica_groups=mesh['blk'=64,'txt'=8] {'txt'}, use_global_device_ids=true, to_apply=%region_9.10 | all-reduce | flops 9344 | bytes 74752 | tf_op jit(solution)/shard_map/psum | solution.py:110
  (979 shorter events, 974.7 us)
Async XLA Ops:
  7.2 1630.9 %all-reduce.4.cloned.1.call-start = ((), (), s32[]{:S(2)}) async-start(), calls=%async_computation | async-start | bytes 4718592
  12.7 14.6 collective-permute-start
  29.9 12.1 collective-permute-start
  46.8 11.1 collective-permute-start
  97.7 10.2 collective-permute-start
  131.5 10.2 collective-permute-start
  182.4 10.2 collective-permute-start
  233.2 10.2 collective-permute-start
  250.2 10.2 collective-permute-start
  301.0 10.2 collective-permute-start
  317.9 10.2 collective-permute-start
  385.7 10.2 collective-permute-start
  436.6 10.2 collective-permute-start
  487.4 10.2 collective-permute-start
  589.1 10.2 collective-permute-start
  639.9 10.2 collective-permute-start
  656.9 10.2 collective-permute-start
  707.7 10.2 collective-permute-start
  758.5 10.2 collective-permute-start
  775.5 10.2 collective-permute-start
  860.2 10.2 collective-permute-start
  894.1 10.2 collective-permute-start
  1046.6 10.2 collective-permute-start
  1063.5 10.2 collective-permute-start
  (176 other events, 1626.7 us)
Sparse Core Ops, SparseCore 0:
  1102.1 535.8 all-reduce.3
where the time goes:
time: 1720 us; the launch traced here: 1700 us
  waiting for transfers between devices  957 us (56%)
  starting transfers between devices  375 us (22%)
  matrix products  203 us (12%)
  local copies, waits for them, and re-layouts  87.6 us (5%)
  blocking collectives  51.2 us (3%)
    unnamed x2, waiting for transfers between devices  533 us
    ppermute x192, waiting for transfers between devices, shifted(): return lax.ppermute(value, axis, pairs)  423 us
    ppermute x192, starting transfers between devices, shifted(): return lax.ppermute(value, axis, pairs)  375 us
    dot_general x128, matrix products, contract_last(): lax.dot_general(first_operand, second_operand, (((1,), (1,)), ((), ())),...  188 us
    psum x1, blocking collectives, shards(): head_rows, loss_rows = lax.psum((head_rows, loss_rows), 'txt')  51.2 us
    slice x64, local copies, waits for them, and re-layouts, pair_tile(): logit_scales[0] * contract_last(text_rows, image_low) + logit_biases[0]  42.1 us
    dynamic_update_slice x64, local copies, waits for them, and re-layouts, record(): lax.dynamic_update_slice(text_store, text_rows, (store_offset, zero_index))  39.1 us
  transfers between devices with their start and end apart: 193, of which 127 were waited for; matrix products, arithmetic and copies ran while one was open for 17% of the time, Pallas kernels for 0%

commit v1 on v0

v1 whole, which is shorter than its diff:
```python
import jax
import jax.numpy as jnp
from jax import lax
from jax.experimental import pallas as pl
from jax.experimental.pallas import tpu as pltpu
from jax.sharding import PartitionSpec as P

epsilon = 1e-06
MESH = pl.DeviceIdType.MESH
f32 = jnp.float32
bf16 = jnp.bfloat16

FLOW = {1: (1, 1), 2: (1, -1), 3: (2, 1), 4: (2, -1), 5: (3, 1), 6: (3, -1), 7: (4, 1)}
NEXT = {1: 3, 2: 4, 3: 5, 4: 6, 5: 7}
GROUPS = [(0, 1), (1, 2), (3, 2), (5, 2), (7, 1)]
ZFLOW = {1: 1, 2: -1, 3: 2}


def contract_last(a, b):
    return lax.dot_general(a, b, (((1,), (1,)), ((), ())), preferred_element_type=f32)


def contract_first(a, b):
    return lax.dot_general(a, b, (((0,), (0,)), ((), ())), preferred_element_type=f32)


class Tags:
    def __init__(self):
        self.index = {}

    def __call__(self, *key):
        return self.index.setdefault(key, len(self.index))


MESSAGES = 128


def kernel(
    x_hbm, w_hbm, ts_hbm, xt_hbm, tt_hbm, scales, biases, loss_scale,
    head_out, text_out, loss_out,
    xall, xtall, w, ts, tt, sb, tb, unit, low, rad, teach, xtp,
    err, town, zs, zr, ysend, yr, grad, sfull, crecv, csum, sx, xr, hsum, hb, hr, zb, zrec, ag, lpart, lc, lx, lxr, lh,
    local_sem, send_sem, recv_sem,
):
    blk = lax.axis_index("blk")
    txt = lax.axis_index("txt")
    x = lax.rem(txt, 4)
    c = lax.rem(blk, 2)
    y = lax.rem(blk // 2, 8)
    z = (txt // 4) * 4 + blk // 16
    sgn = 2 * c - 1

    def at(dx=0, dy=0, dz=0, core=c):
        xx = lax.rem(x + dx + 8, 4)
        yy = lax.rem(y + dy + 16, 8)
        zz = lax.rem(z + dz + 16, 8)
        return {"blk": (lax.rem(zz, 4) * 8 + yy) * 2 + core, "txt": (zz // 4) * 4 + xx}

    loads = [
        pltpu.make_async_copy(ts_hbm, ts, local_sem.at[0]),
        pltpu.make_async_copy(tt_hbm, tt, local_sem.at[1]),
        pltpu.make_async_copy(x_hbm, xall.at[c], local_sem.at[2]),
        pltpu.make_async_copy(xt_hbm, xtall.at[c], local_sem.at[3]),
        pltpu.make_async_copy(w_hbm, w, local_sem.at[4]),
    ]
    for copy in loads:
        copy.start()

    barrier = pltpu.get_barrier_semaphore()
    partners = [at(core=1 - c)]
    partners += [at(dx=r, core=k) for r in (1, 2, 3) for k in (c, 1 - c)]
    partners += [at(dy=r) for r in range(1, 8)]
    partners += [at(dz=r) for r in range(1, 8)]
    for partner in partners:
        pl.semaphore_signal(barrier, inc=1, device_id=partner, device_id_type=MESH)

    tags = Tags()

    def message(key, src, dst, device):
        index = tags(*key)
        assert index < MESSAGES
        return pltpu.make_async_remote_copy(
            src, dst, send_sem.at[index], recv_sem.at[index], device_id=device, device_id_type=MESH
        )

    sent = []

    def send(key, src, dst, device):
        copy = message(key, src, dst, device)
        copy.start()
        sent.append(copy)

    def arrive(key, dst):
        message(key, dst, dst, at()).wait_recv()

    loads[0].wait()
    loads[1].wait()
    t_wide = ts[...].astype(f32)
    t_rad = jnp.sqrt(jnp.sum(t_wide * t_wide, axis=1, keepdims=True) + epsilon)
    t_unit = t_wide / t_rad
    sb[0, 0] = t_unit.astype(bf16)
    q_wide = tt[...].astype(f32)
    tb[0, 0] = (q_wide / jnp.sqrt(jnp.sum(q_wide * q_wide, axis=1, keepdims=True) + epsilon)).astype(bf16)

    pl.semaphore_wait(barrier, len(partners))

    y_to = {1: at(dy=sgn), -1: at(dy=-sgn)}
    z_to = {1: at(dz=sgn), -1: at(dz=-sgn)}
    sibling = at(core=1 - c)

    def s_part(pos, part):
        return sb.at[pos, pl.ds(0, 1)] if part == 0 else sb.at[pos, pl.ds(1, 2)] if part == 1 else sb.at[pos, pl.ds(3, 1)]

    def t_group(b, group):
        start, count = GROUPS[group]
        return tb.at[b, pl.ds(start, count)]

    def send_s_y(pos_from, part):
        targets = [(1, 1), (2, -1)] if pos_from == 0 else [(NEXT[pos_from], FLOW[pos_from][1])] if pos_from in NEXT else []
        for pos, sign in targets:
            send(("sy", pos, part), s_part(pos_from, part), s_part(pos, part), y_to[sign])

    def send_t_y(pos_from):
        targets = [(1, 1), (2, -1)] if pos_from == 0 else [(NEXT[pos_from], FLOW[pos_from][1])] if pos_from in NEXT else []
        for pos, sign in targets:
            send(("ty", pos), tb.at[0, pos_from], tb.at[0, pos], y_to[sign])

    def send_t_z(group):
        send(("tz", 1, group), t_group(0, group), t_group(1, group), z_to[1])
        send(("tz", 2, group), t_group(0, group), t_group(2, group), z_to[-1])

    send_t_y(0)
    send(("sz", 1), sb.at[0, 0], sb.at[0, 1], z_to[1])
    send(("sz", 2), sb.at[0, 0], sb.at[0, 2], z_to[-1])
    send_s_y(0, 0)
    send_t_z(0)
    loads[2].wait()
    loads[3].wait()
    send(("imgs",), xall.at[c], xall.at[c], sibling)
    send(("imgt",), xtall.at[c], xtall.at[c], sibling)

    def prepare(k):
        projected = jnp.dot(xall[k], w[...], preferred_element_type=f32)
        radius = jnp.sqrt(jnp.sum(projected * projected, axis=1, keepdims=True) + epsilon)
        u = projected / radius
        unit[k] = u
        rad[k] = radius
        low[k] = u.astype(bf16)
        v = xtall[k].astype(f32)
        teach[k] = (v / jnp.sqrt(jnp.sum(v * v, axis=1, keepdims=True) + epsilon)).astype(bf16)

    def turn():
        for k in range(2):
            flat = xall[k].astype(f32).T
            for yy in range(8):
                rows = [flat[zl * 192 + yy * 24 : zl * 192 + yy * 24 + 24] for zl in range(4)]
                xtp[yy, :, 128 * k : 128 * (k + 1)] = jnp.concatenate(rows, axis=0).astype(bf16)

    def hop(h):
        for pos in range(1, 8):
            if FLOW[pos][0] == h:
                arrive(("ty", pos), tb.at[0, pos])
                send_t_y(pos)
        if h <= 4:
            send_t_z(h)
        if h == 1:
            arrive(("sz", 1), sb.at[0, 1])
            send(("sz", 3), sb.at[0, 1], sb.at[0, 3], z_to[1])
            arrive(("sz", 2), sb.at[0, 2])
            send_s_y(0, 1)
        if h == 2:
            arrive(("sz", 3), sb.at[0, 3])
            send_s_y(0, 2)
        for part in range(3):
            for pos in range(1, 8):
                if FLOW[pos][0] + part == h:
                    arrive(("sy", pos, part), s_part(pos, part))
                    send_s_y(pos, part)
        if 0 <= h - 1 <= 4:
            group = h - 1
            arrive(("tz", 1, group), t_group(1, group))
            send(("tz", 3, group), t_group(1, group), t_group(3, group), z_to[1])
            arrive(("tz", 2, group), t_group(2, group))
        if 0 <= h - 2 <= 4:
            group = h - 2
            arrive(("tz", 3, group), t_group(3, group))

    def tile(group):
        start, count = GROUPS[group]
        n = count * 64
        rows = sb[start : start + count].reshape(n, 768)
        teach_rows = jnp.concatenate([tb[:, p].reshape(64, 1152) for p in range(start, start + count)], axis=0)
        low_all = low[...].reshape(256, 768)
        student = scales[0] * contract_last(rows, low_all) + biases[0]
        teacher = scales[1] * contract_last(teach_rows, teach[...].reshape(256, 1152)) + biases[1]
        target = 1.0 / (1.0 + jnp.exp(-teacher))
        small = jnp.exp(-jnp.abs(student))
        inverse = 1.0 / (1.0 + small)
        sig = jnp.where(student >= 0.0, inverse, small * inverse)
        loss = jnp.maximum(student, 0.0) + jnp.log1p(small) - target * student
        errors = (sig - target).astype(bf16)
        part = jnp.sum(loss, axis=0, keepdims=True)
        gradient = contract_first(errors, rows)
        if group == 0:
            lpart[...] = part
            grad[...] = gradient
        else:
            lpart[...] += part
            grad[...] += gradient
        term = jnp.dot(errors, low_all, preferred_element_type=f32).reshape(count, 4, 16, 768)
        town[start : start + count] = term[:, 0]
        for b in (1, 2, 3):
            zs[b - 1, start : start + count] = term[:, b].astype(bf16)

    def back_z(group):
        start, count = GROUPS[group]
        for b in (1, 2, 3):
            here = pl.ds(start, count)
            send(("gz", b, group), zs.at[b - 1, here], zr.at[b - 1, here], at(dz=-ZFLOW[b] * sgn))

    def back_y(group):
        start, count = GROUPS[group]
        here = pl.ds(start, count)
        for b in (1, 2, 3):
            arrive(("gz", b, group), zr.at[b - 1, here])
        total = town[start : start + count]
        for b in range(3):
            total = total + zr[b, start : start + count].astype(f32)
        town[start : start + count] = total
        for pos in range(start, start + count):
            if pos:
                steps, sign = FLOW[pos]
                send(("gy", pos), town.at[pos], yr.at[pos], at(dy=-steps * sign * sgn))

    loads[4].wait()
    hop(1)
    arrive(("imgs",), xall.at[1 - c])
    arrive(("imgt",), xtall.at[1 - c])
    prepare(0)
    hop(2)
    prepare(1)
    tile(0)
    back_z(0)
    hop(3)
    tile(1)
    back_z(1)
    back_y(0)
    hop(4)
    tile(2)
    back_z(2)
    back_y(1)
    hop(5)
    tile(3)
    back_z(3)
    back_y(2)
    turn()
    hop(6)
    tile(4)

    factor = loss_scale[0] * scales[0] / 8192.0
    g = grad[...] * factor
    u = unit[...].reshape(256, 768)
    step = (g - u * jnp.sum(g * u, axis=1, keepdims=True)) / rad[...].reshape(256, 1)
    for j in range(6):
        sfull[j] = step[:, 128 * j : 128 * (j + 1)]
    for k in range(2):
        lc[k] = jnp.broadcast_to(lpart[:, 128 * k : 128 * (k + 1)], (8, 128))
    send(("cs",), sfull.at[pl.ds(3 * (1 - c), 3)], crecv, sibling)
    send(("cl",), lc.at[1 - c], lc.at[2], sibling)
    back_z(4)
    back_y(3)

    arrive(("cs",), crecv)
    total = sfull[pl.ds(3 * c, 3)] + crecv[...]
    csum[...] = total
    sx[...] = total.astype(bf16)
    for r in (1, 2, 3):
        xto = lax.rem(x + r, 4)
        copy = message(("xs", r), sx.at[lax.rem(xto, 3)], xr.at[r - 1], at(dx=r))

        @pl.when(xto < 3)
        def _():
            copy.start()

    arrive(("cl",), lc.at[2])
    lx[...] = lc[c] + lc[2]
    for r in (1, 2, 3):
        send(("xl", r), lx, lxr.at[r - 1], at(dx=r))
    back_y(4)

    @pl.when(x < 3)
    def _():
        for r in (1, 2, 3):
            arrive(("xs", r), xr.at[r - 1])
        s = csum[x] + xr[0].astype(f32) + xr[1].astype(f32) + xr[2].astype(f32)
        high = s.astype(bf16)
        rest = (s - high.astype(f32)).astype(bf16)
        both = jnp.dot(xtp[...].reshape(768, 256), jnp.concatenate([high, rest], axis=1), preferred_element_type=f32)
        h = (both[:, :128] + both[:, 128:]).reshape(8, 96, 128)
        hsum[...] = h
        hb[...] = h.astype(bf16)
        for r in range(1, 8):
            message(("hy", r), hb.at[lax.rem(y + r, 8)], hr.at[r - 1], at(dy=r)).start()

    for r in (1, 2, 3):
        arrive(("xl", r), lxr.at[r - 1])
    lh[0] = lx[...] + lxr[0] + lxr[1] + lxr[2]
    send(("hl",), lh.at[0], lh.at[1], at(dz=4))

    for pos in range(1, 8):
        arrive(("gy", pos), yr.at[pos])
    tg = town[0]
    for pos in range(1, 8):
        tg = tg + yr[pos]
    tg = tg * factor
    tw = ts[...].astype(f32)
    tr = jnp.sqrt(jnp.sum(tw * tw, axis=1, keepdims=True) + epsilon)
    tu = tw / tr
    text_out[...] = (tg - tu * jnp.sum(tg * tu, axis=1, keepdims=True)) / tr

    @pl.when(x < 3)
    def _():
        for r in range(1, 8):
            arrive(("hy", r), hr.at[r - 1])
        total = hsum[y]
        for r in range(1, 8):
            total = total + hr[r - 1].astype(f32)
        zb[...] = total.reshape(4, 24, 128)
        for r in range(1, 8):
            message(("hz", r), zb.at[lax.rem(z + r, 4)], zrec.at[r - 1], at(dz=r)).start()

    arrive(("hl",), lh.at[1])
    loss_out[...] = (lh[0, 0:1] + lh[1, 0:1]) * (1.0 / 8192.0)

    mine = 3 * c + lax.rem(x, 3)

    @pl.when(x < 3)
    def _():
        for r in range(1, 8):
            arrive(("hz", r), zrec.at[r - 1])
        total = zb[lax.rem(z, 4)]
        for r in range(1, 8):
            total = total + zrec[r - 1]
        ag[mine] = total
        message(("agc",), ag.at[mine], ag.at[mine], sibling).start()
        for r in (1, 2, 3):
            for k in (0, 1):
                message(("agx", r, k), ag.at[mine], ag.at[mine], at(dx=r, core=c if k == 0 else 1 - c)).start()
        arrive(("agc",), ag.at[0])

    for r in (1, 2, 3):
        for k in (0, 1):

            @pl.when(lax.rem(x - r + 4, 4) < 3)
            def _(r=r, k=k):
                arrive(("agx", r, k), ag.at[0])

    for j in range(6):
        head_out[:, 128 * j : 128 * (j + 1)] = jnp.where(c == 0, ag[j, 0:12], ag[j, 12:24])

    for copy in sent:
        copy.wait_send()
    for r in (1, 2, 3):
        xto = lax.rem(x + r, 4)
        copy = message(("xs", r), sx.at[0], xr.at[r - 1], at(dx=r))

        @pl.when(xto < 3)
        def _():
            copy.wait_send()

    @pl.when(x < 3)
    def _():
        for r in range(1, 8):
            message(("hy", r), hb.at[0], hr.at[r - 1], at()).wait_send()
            message(("hz", r), zb.at[0], zrec.at[r - 1], at()).wait_send()
        message(("agc",), ag.at[0], ag.at[0], at()).wait_send()
        for r in (1, 2, 3):
            for k in (0, 1):
                message(("agx", r, k), ag.at[0], ag.at[0], at()).wait_send()


def shards(image_student, head_weight, text_student, image_teacher, text_teacher, logit_scales, logit_biases, loss_scale):
    vm = pltpu.VMEM
    scratch = [
        vm((2, 128, 768), bf16),
        vm((2, 128, 1152), bf16),
        vm((768, 768), bf16),
        vm((16, 768), bf16),
        vm((16, 1152), bf16),
        vm((8, 4, 16, 768), bf16),
        vm((4, 8, 16, 1152), bf16),
        vm((2, 128, 768), f32),
        vm((2, 128, 768), bf16),
        vm((2, 128, 1), f32),
        vm((2, 128, 1152), bf16),
        vm((8, 96, 256), bf16),
        vm((8, 128), f32),
        vm((8, 16, 768), f32),
        vm((3, 8, 16, 768), bf16),
        vm((3, 8, 16, 768), bf16),
        vm((8, 128), f32),
        vm((8, 16, 768), f32),
        vm((256, 768), f32),
        vm((6, 256, 128), f32),
        vm((3, 256, 128), f32),
        vm((3, 256, 128), f32),
        vm((3, 256, 128), bf16),
        vm((3, 256, 128), bf16),
        vm((8, 96, 128), f32),
        vm((8, 96, 128), bf16),
        vm((7, 96, 128), bf16),
        vm((4, 24, 128), f32),
        vm((7, 24, 128), f32),
        vm((6, 24, 128), f32),
        vm((1, 256), f32),
        vm((3, 8, 128), f32),
        vm((8, 128), f32),
        vm((3, 8, 128), f32),
        vm((2, 8, 128), f32),
        pltpu.SemaphoreType.DMA((5,)),
        pltpu.SemaphoreType.DMA((MESSAGES,)),
        pltpu.SemaphoreType.DMA((MESSAGES,)),
    ]
    any_spec = pl.BlockSpec(memory_space=pl.ANY)
    smem = pl.BlockSpec(memory_space=pltpu.SMEM)
    vmem = pl.BlockSpec(memory_space=pltpu.VMEM)
    head, text, loss = pl.pallas_call(
        kernel,
        out_shape=(
            jax.ShapeDtypeStruct((12, 768), f32),
            jax.ShapeDtypeStruct((16, 768), f32),
            jax.ShapeDtypeStruct((1, 128), f32),
        ),
        in_specs=[any_spec] * 5 + [smem] * 3,
        out_specs=(vmem, vmem, vmem),
        scratch_shapes=scratch,
        compiler_params=pltpu.CompilerParams(collective_id=0, has_side_effects=True, vmem_limit_bytes=48 * 1024 * 1024),
        name="distill",
    )(image_student, head_weight, text_student, image_teacher, text_teacher, logit_scales, logit_biases, loss_scale)
    return head, text, loss.reshape(128)


def solution(mesh):
    placed = (
        P("blk", None), P(), P(("blk", "txt"), None), P("blk", None), P(("blk", "txt"), None), P(), P(), P(),
    )
    return jax.shard_map(
        shards,
        mesh=mesh,
        in_specs=placed,
        out_specs=(P("blk", None), P(("blk", "txt"), None), P("blk")),
        check_vma=False,
    )
```

time: 1720 us -> 76.6 us (0.04); the launches traced: 1700 us -> 76.2 us
  waiting for transfers between devices: 957 us -> 0 us
  starting transfers between devices: 375 us -> 0 us
  matrix products: 203 us -> 0 us
  local copies, waits for them, and re-layouts: 87.6 us -> 7.72 us
  Pallas kernels: 0 us -> 67.2 us
  blocking collectives: 51.2 us -> 0 us
    unnamed x2 -> x0, waiting for transfers between devices: 533 us -> none
    ppermute x192 -> x0, waiting for transfers between devices: 423 us -> none  [shifted(): return lax.ppermute(value, axis, pairs)]
    ppermute x192 -> x0, starting transfers between devices: 375 us -> none  [shifted(): return lax.ppermute(value, axis, pairs)]
    dot_general x195 -> x0, matrix products: 203 us -> none  [the longest x128 188 us: contract_last(): lax.dot_general(first_operand, second_operand, (((1,), (1,)), ((), ())),...]
    pallas_call x0 -> x1, Pallas kernels: none -> 67.2 us  [shards(): pl.pallas_call(kernel, out_shape=(jax.ShapeDtypeStruct((12, 768), f32), j...]
    psum x1 -> x0, blocking collectives: 51.2 us -> none  [shards(): head_rows, loss_rows = lax.psum((head_rows, loss_rows), 'txt')]
    slice x64 -> x0, local copies, waits for them, and re-layouts: 42.1 us -> none  [pair_tile(): logit_scales[0] * contract_last(text_rows, image_low) + logit_biases[0]]
    dynamic_update_slice x64 -> x0, local copies, waits for them, and re-layouts: 39.1 us -> none  [record(): lax.dynamic_update_slice(text_store, text_rows, (store_offset, zero_index))]
  transfers between devices with their start and end apart: 193 -> 0, of which waited for: 127 -> 0; matrix products, arithmetic and copies ran while one was open for 17% -> 0% of each run, Pallas kernels for 0% -> 0%
where the time goes in v1:
time: 76.6 us; the launch traced here: 76.2 us
  Pallas kernels  67.2 us (88%)
  local copies, waits for them, and re-layouts  7.72 us (10%)
  between operations  1.3 us (2%)
    pallas_call x1, Pallas kernels, shards(): pl.pallas_call(kernel, out_shape=(jax.ShapeDtypeStruct((12, 768), f32), j...  67.2 us
    unnamed x17, local copies, waits for them, and re-layouts  7.72 us

profile of v1, /device:TPU:1, one launch (start us, length us, event | category | flops | bytes accessed | tf_op | source)
XLA Modules:
  0.0 76.2 jit_solution(412532436497847009)
XLA Ops:
  1.3 0.0 copy-start
  1.3 1.3 %copy-done = bf16[768,768]{1,0:T(8,128)(2,1)S(1)} copy-done((bf16[768,768]{1,0:T(8,128)(2,1)S(1)}, bf16[768,768]{1,0:T(8,128)(2,1)}, u32[]{:S(2)}) %copy-start) | copy-done | bytes 1179672
  2.6 0.0 copy-start.1
  2.6 1.0 %copy-done.1 = bf16[128,1152]{1,0:T(8,128)(2,1)S(1)} copy-done((bf16[128,1152]{1,0:T(8,128)(2,1)S(1)}, bf16[128,1152]{1,0:T(8,128)(2,1)}, u32[]{:S(2)}) %copy-start.1) | copy-done | bytes 294936
  3.5 0.0 copy-start.2
  3.5 0.9 %copy-done.2 = bf16[128,768]{1,0:T(8,128)(2,1)S(1)} copy-done((bf16[128,768]{1,0:T(8,128)(2,1)S(1)}, bf16[128,768]{1,0:T(8,128)(2,1)}, u32[]{:S(2)}) %copy-start.2) | copy-done | bytes 196632
  4.4 0.0 copy-start.3
  4.4 0.8 %copy-done.3 = bf16[16,1152]{1,0:T(8,128)(2,1)S(1)} copy-done((bf16[16,1152]{1,0:T(8,128)(2,1)S(1)}, bf16[16,1152]{1,0:T(8,128)(2,1)}, u32[]{:S(2)}) %copy-start.3) | copy-done | bytes 36888
  5.2 0.0 copy-start.4
  5.2 0.7 copy-done.4
  5.9 0.0 copy-start.5
  5.9 0.7 copy-done.5
  6.6 0.0 copy-start.6
  6.6 0.7 copy-done.6
  7.3 67.2 %distill.1 = (f32[12,768]{1,0:T(8,128)S(1)}, f32[16,768]{1,0:T(8,128)S(1)}, f32[1,128]{1,0:T(1,128)S(1)}) custom-call(bf16[128,768]{1,0:T(8,128)(2,1)S(1)} %copy-done.2, bf16[768,768]{1,0:T(8,128)(2,1)S(1)} %copy-done, bf16[16,768]{1,0:T(8,128)(2,1)S(1)} %copy-done.4, bf16[128,1152]{1,0:T(8,128)(2,1)S(1)} %copy-done.1, bf16[16,1152]{1,0:T(8,128)(2,1)S(1)} %copy-done.3, ...), custom_call_target="tpu_custom_call" | custom-call | tf_op jit(solution)/shard_map/distill/pallas_call | solution.py:427
  74.4 0.6 copy.15
  75.1 0.6 copy.16
  75.7 0.5 copy.17
Async XLA Ops:
  1.3 1.3 %copy-start = (bf16[768,768]{1,0:T(8,128)(2,1)S(1)}, bf16[768,768]{1,0:T(8,128)(2,1)}, u32[]{:S(2)}) copy-start(bf16[768,768]{1,0:T(8,128)(2,1)} %w_hbm.1) | copy-start | bytes 3538948
  2.6 1.0 %copy-start.1 = (bf16[128,1152]{1,0:T(8,128)(2,1)S(1)}, bf16[128,1152]{1,0:T(8,128)(2,1)}, u32[]{:S(2)}) copy-start(bf16[128,1152]{1,0:T(8,128)(2,1)} %xt_hbm.1) | copy-start | bytes 884740
  3.5 0.9 %copy-start.2 = (bf16[128,768]{1,0:T(8,128)(2,1)S(1)}, bf16[128,768]{1,0:T(8,128)(2,1)}, u32[]{:S(2)}) copy-start(bf16[128,768]{1,0:T(8,128)(2,1)} %x_hbm.1) | copy-start | bytes 589828
  4.4 0.8 %copy-start.3 = (bf16[16,1152]{1,0:T(8,128)(2,1)S(1)}, bf16[16,1152]{1,0:T(8,128)(2,1)}, u32[]{:S(2)}) copy-start(bf16[16,1152]{1,0:T(8,128)(2,1)} %tt_hbm.1) | copy-start | bytes 110596
  5.2 0.7 copy-start.4
  5.9 0.7 copy-start.5
  6.6 0.7 copy-start.6

commit v2 on v1

v2 whole, which is shorter than its diff:
```python
import math

import jax
import jax.numpy as jnp
from jax import lax
from jax.experimental import pallas as pl
from jax.experimental.pallas import tpu as pltpu
from jax.sharding import PartitionSpec as P

epsilon = 1e-06
MESH = pl.DeviceIdType.MESH
f32 = jnp.float32
bf16 = jnp.bfloat16

FLOW = {1: (1, 1), 2: (1, -1), 3: (2, 1), 4: (2, -1), 5: (3, 1), 6: (3, -1), 7: (4, 1)}
NEXT = {1: 3, 2: 4, 3: 5, 4: 6, 5: 7}
GROUPS = [(0, 1), (1, 2), (3, 2), (5, 2), (7, 1)]
ZFLOW = {1: 1, 2: -1, 3: 2}


def contract_last(a, b):
    return lax.dot_general(a, b, (((1,), (1,)), ((), ())), preferred_element_type=f32)


def contract_first(a, b):
    return lax.dot_general(a, b, (((0,), (0,)), ((), ())), preferred_element_type=f32)


class Tags:
    def __init__(self):
        self.index = {}

    def __call__(self, key):
        return self.index.setdefault(key, len(self.index))


MESSAGES = 56
ROOM = 2048


def kernel(
    x_hbm, w_hbm, ts_hbm, xt_hbm, tt_hbm, scales_hbm, biases_hbm, loss_scale_hbm,
    head_out, text_out, loss_out,
    xall, xtall, w, ts, tt, sb, tb, unit, low, rad, teach, xtp,
    town, zs, zr, ysend, yr, grad, sfull, crecv, csum, sx, xr, hsum, hb, hr, zb, zrec, ag, lpart, lc, lx, lxr, lh,
    room, scales, biases, loss_scale, local_sem, send_sem, recv_sem,
):
    blk = lax.axis_index("blk")
    txt = lax.axis_index("txt")
    x = lax.rem(txt, 4)
    c = lax.rem(blk, 2)
    y = lax.rem(blk // 2, 8)
    z = (txt // 4) * 4 + blk // 16
    sgn = 2 * c - 1

    def at(dx=0, dy=0, dz=0, core=c):
        xx = lax.rem(x + dx + 8, 4)
        yy = lax.rem(y + dy + 16, 8)
        zz = lax.rem(z + dz + 16, 8)
        return {"blk": (lax.rem(zz, 4) * 8 + yy) * 2 + core, "txt": (zz // 4) * 4 + xx}

    barrier = pltpu.get_barrier_semaphore()
    partners = [at(core=1 - c)]
    partners += [at(dy=1), at(dy=-1), at(dz=1), at(dz=-1)]
    partners += [at(dz=-2 * sgn)] + [at(dx=r) for r in (1, 2, 3)]
    for partner in partners:
        pl.semaphore_signal(barrier, inc=1, device_id=partner, device_id_type=MESH)

    loads = [
        pltpu.make_async_copy(ts_hbm, ts, local_sem.at[0]),
        pltpu.make_async_copy(tt_hbm, tt, local_sem.at[1]),
        pltpu.make_async_copy(x_hbm, xall.at[c], local_sem.at[2]),
        pltpu.make_async_copy(xt_hbm, xtall.at[c], local_sem.at[3]),
        pltpu.make_async_copy(w_hbm, w, local_sem.at[4]),
        pltpu.make_async_copy(scales_hbm, scales, local_sem.at[5]),
        pltpu.make_async_copy(biases_hbm, biases, local_sem.at[6]),
        pltpu.make_async_copy(loss_scale_hbm, loss_scale, local_sem.at[7]),
    ]
    for copy in loads:
        copy.start()

    tags = Tags()
    left = {}

    def send(key, src, dst, device, lane=0):
        index = tags(key)
        assert index < MESSAGES
        pltpu.make_async_remote_copy(
            src, dst, send_sem.at[lane], recv_sem.at[index], device_id=device, device_id_type=MESH
        ).start()
        left[lane] = left.get(lane, 0) + math.prod(src.shape) * src.dtype.itemsize // 4096

    def arrive(key, dst):
        sem = recv_sem.at[tags(key)]
        pltpu.make_async_remote_copy(dst, dst, send_sem.at[0], sem, device_id=sibling, device_id_type=MESH).wait_recv()

    def gone(lane, units):
        view = room.at[pl.ds(0, units)]
        sem = send_sem.at[lane]
        pltpu.make_async_remote_copy(view, view, sem, recv_sem.at[0], device_id=sibling, device_id_type=MESH).wait_send()

    sibling = at(core=1 - c)

    loads[0].wait()
    loads[1].wait()
    t_wide = ts[...].astype(f32)
    t_rad = jnp.sqrt(jnp.sum(t_wide * t_wide, axis=1, keepdims=True) + epsilon)
    t_unit = t_wide / t_rad
    sb[0, 0] = t_unit.astype(bf16)
    q_wide = tt[...].astype(f32)
    tb[0, 0] = (q_wide / jnp.sqrt(jnp.sum(q_wide * q_wide, axis=1, keepdims=True) + epsilon)).astype(bf16)

    pl.semaphore_wait(barrier, len(partners))

    y_to = {1: at(dy=sgn), -1: at(dy=-sgn)}
    z_to = {1: at(dz=sgn), -1: at(dz=-sgn)}

    def s_part(pos, part):
        return sb.at[pos, pl.ds(0, 1)] if part == 0 else sb.at[pos, pl.ds(1, 2)] if part == 1 else sb.at[pos, pl.ds(3, 1)]

    def t_group(b, group):
        start, count = GROUPS[group]
        return tb.at[b, pl.ds(start, count)]

    def send_s_y(pos_from, part):
        targets = [(1, 1), (2, -1)] if pos_from == 0 else [(NEXT[pos_from], FLOW[pos_from][1])] if pos_from in NEXT else []
        for pos, sign in targets:
            send(("sy", pos, part), s_part(pos_from, part), s_part(pos, part), y_to[sign])

    def send_t_y(pos_from):
        targets = [(1, 1), (2, -1)] if pos_from == 0 else [(NEXT[pos_from], FLOW[pos_from][1])] if pos_from in NEXT else []
        for pos, sign in targets:
            send(("ty", pos), tb.at[0, pos_from], tb.at[0, pos], y_to[sign])

    def send_t_z(group):
        send(("tz", 1, group), t_group(0, group), t_group(1, group), z_to[1])
        send(("tz", 2, group), t_group(0, group), t_group(2, group), z_to[-1])

    send_t_y(0)
    send(("sz", 1), sb.at[0, 0], sb.at[0, 1], z_to[1])
    send(("sz", 1), sb.at[0, 0], sb.at[0, 2], z_to[-1])
    send(("sz", 3), sb.at[0, 0], sb.at[0, 3], at(dz=2 * sgn))
    send_s_y(0, 0)
    send_t_z(0)
    loads[2].wait()
    loads[3].wait()
    send("imgs", xall.at[c], xall.at[c], sibling)
    send("imgt", xtall.at[c], xtall.at[c], sibling)

    def prepare(k):
        projected = jnp.dot(xall[k], w[...], preferred_element_type=f32)
        radius = jnp.sqrt(jnp.sum(projected * projected, axis=1, keepdims=True) + epsilon)
        u = projected / radius
        unit[k] = u
        rad[k] = radius
        low[k] = u.astype(bf16)
        v = xtall[k].astype(f32)
        teach[k] = (v / jnp.sqrt(jnp.sum(v * v, axis=1, keepdims=True) + epsilon)).astype(bf16)

    def turn():
        for k in range(2):
            flat = xall[k].astype(f32).T
            for yy in range(8):
                rows = [flat[zl * 192 + yy * 24 : zl * 192 + yy * 24 + 24] for zl in range(4)]
                xtp[yy, :, 128 * k : 128 * (k + 1)] = jnp.concatenate(rows, axis=0).astype(bf16)

    def hop(h):
        for pos in range(1, 8):
            if FLOW[pos][0] == h:
                arrive(("ty", pos), tb.at[0, pos])
                send_t_y(pos)
        if h <= 4:
            send_t_z(h)
        if h == 1:
            arrive(("sz", 1), s_part(0, 1))
            send_s_y(0, 1)
        if h == 2:
            arrive(("sz", 3), sb.at[0, 3])
            send_s_y(0, 2)
        for part in range(3):
            for pos in range(1, 8):
                if FLOW[pos][0] + part == h:
                    arrive(("sy", pos, part), s_part(pos, part))
                    send_s_y(pos, part)
        if 0 <= h - 1 <= 4:
            group = h - 1
            arrive(("tz", 1, group), t_group(1, group))
            send(("tz", 2, group), t_group(1, group), t_group(3, group), z_to[1])

    def tile(group):
        start, count = GROUPS[group]
        arrive(("tz", 2, group), tb.at[pl.ds(2, 2), pl.ds(start, count)])
        n = count * 64
        rows = sb[start : start + count].reshape(n, 768)
        teach_rows = jnp.concatenate([tb[:, p].reshape(64, 1152) for p in range(start, start + count)], axis=0)
        low_all = low[...].reshape(256, 768)
        student = scales[0] * contract_last(rows, low_all) + biases[0]
        teacher = scales[1] * contract_last(teach_rows, teach[...].reshape(256, 1152)) + biases[1]
        target = 1.0 / (1.0 + jnp.exp(-teacher))
        small = jnp.exp(-jnp.abs(student))
        inverse = 1.0 / (1.0 + small)
        sig = jnp.where(student >= 0.0, inverse, small * inverse)
        loss = jnp.maximum(student, 0.0) + jnp.log1p(small) - target * student
        errors = (sig - target).astype(bf16)
        part = jnp.sum(loss, axis=0, keepdims=True)
        gradient = contract_first(errors, rows)
        if group == 0:
            lpart[...] = part
            grad[...] = gradient
        else:
            lpart[...] += part
            grad[...] += gradient
        term = jnp.dot(errors, low_all, preferred_element_type=f32).reshape(count, 4, 16, 768)
        town[start : start + count] = term[:, 0]
        for b in (1, 2, 3):
            zs[b - 1, start : start + count] = term[:, b].astype(bf16)

    def back_z():
        for b in (3, 1, 2):
            send("gz", zs.at[b - 1], zr.at[b - 1], at(dz=-ZFLOW[b] * sgn))

    def sum_z():
        arrive("gz", zr)
        total = town[...]
        for b in range(3):
            total = total + zr[b].astype(f32)
        town[...] = total
        ysend[...] = total.astype(bf16)

    def back_y(pos):
        steps, sign = FLOW[pos]
        send("gy", ysend.at[pos], yr.at[pos - 1], at(dy=-steps * sign * sgn))

    for copy in loads[4:]:
        copy.wait()
    hop(1)
    arrive("imgs", xall.at[1 - c])
    arrive("imgt", xtall.at[1 - c])
    prepare(0)
    hop(2)
    prepare(1)
    hop(3)
    tile(0)
    hop(4)
    tile(1)
    hop(5)
    tile(2)
    turn()
    tile(3)
    hop(6)
    tile(4)

    factor = loss_scale[0] * scales[0] / 8192.0
    g = grad[...] * factor
    u = unit[...].reshape(256, 768)
    step = (g - u * jnp.sum(g * u, axis=1, keepdims=True)) / rad[...].reshape(256, 1)
    for j in range(6):
        sfull[j] = step[:, 128 * j : 128 * (j + 1)]
    for k in range(2):
        lc[k] = jnp.broadcast_to(lpart[:, 128 * k : 128 * (k + 1)], (8, 128))
    send("cs", sfull.at[pl.ds(3 * (1 - c), 3)], crecv, sibling)
    send("cl", lc.at[1 - c], lc.at[2], sibling)
    back_z()

    arrive("cs", crecv)
    total = sfull[pl.ds(3 * c, 3)] + crecv[...]
    csum[...] = total
    sx[...] = total.astype(bf16)
    for r in (1, 2, 3):
        xto = lax.rem(x + r, 4)

        @pl.when(xto < 3)
        def _():
            send("xs", sx.at[lax.rem(xto, 3)], xr.at[r - 1], at(dx=r), lane=r)

    arrive("cl", lc.at[2])
    lx[...] = lc[c] + lc[2]
    for r in (1, 2, 3):
        send("xl", lx, lxr.at[r - 1], at(dx=r))

    @pl.when(x < 3)
    def _():
        arrive("xs", xr)
        s = csum[x] + xr[0].astype(f32) + xr[1].astype(f32) + xr[2].astype(f32)
        high = s.astype(bf16)
        rest = (s - high.astype(f32)).astype(bf16)
        both = jnp.dot(xtp[...].reshape(768, 256), jnp.concatenate([high, rest], axis=1), preferred_element_type=f32)
        h = (both[:, :128] + both[:, 128:]).reshape(8, 96, 128)
        hsum[...] = h
        hb[...] = h.astype(bf16)
        for r in range(1, 8):
            send("hy", hb.at[lax.rem(y + r, 8)], hr.at[r - 1], at(dy=r), lane=4)

    arrive("xl", lxr)
    lh[0] = lx[...] + lxr[0] + lxr[1] + lxr[2]
    send("hl", lh.at[0], lh.at[1], at(dz=4))
    sum_z()

    @pl.when(x < 3)
    def _():
        arrive("hy", hr)
        total = hsum[y]
        for r in range(1, 8):
            total = total + hr[r - 1].astype(f32)
        zb[...] = total.reshape(4, 24, 128)
        for r in range(1, 8):
            send("hz", zb.at[lax.rem(z + r, 4)], zrec.at[r - 1], at(dz=r), lane=4)

    for pos in range(7, 0, -1):
        back_y(pos)
    arrive("hl", lh.at[1])
    loss_out[...] = (lh[0, 0:1] + lh[1, 0:1]) * (1.0 / 8192.0)

    mine = 3 * c + lax.rem(x, 3)

    @pl.when(x < 3)
    def _():
        arrive("hz", zrec)
        total = zb[lax.rem(z, 4)]
        for r in range(1, 8):
            total = total + zrec[r - 1]
        ag[mine] = total
        send("ag", ag.at[mine], ag.at[mine], sibling, lane=4)
        for r in (1, 2, 3):
            for k in (0, 1):
                send("ag", ag.at[mine], ag.at[mine], at(dx=r, core=c if k == 0 else 1 - c), lane=4)

    arrive("gy", yr)
    tg = town[0]
    for pos in range(1, 8):
        tg = tg + yr[pos - 1].astype(f32)
    tg = tg * factor
    tw = ts[...].astype(f32)
    tr = jnp.sqrt(jnp.sum(tw * tw, axis=1, keepdims=True) + epsilon)
    tu = tw / tr
    text_out[...] = (tg - tu * jnp.sum(tg * tu, axis=1, keepdims=True)) / tr

    @pl.when(x < 3)
    def _():
        arrive("ag", ag.at[pl.ds(0, 5)])

    @pl.when(x == 3)
    def _():
        arrive("ag", ag)

    for j in range(6):
        head_out[:, 128 * j : 128 * (j + 1)] = jnp.where(c == 0, ag[j, 0:12], ag[j, 12:24])

    gone(0, left[0])
    for r in (1, 2, 3):

        @pl.when(lax.rem(x + r, 4) < 3)
        def _():
            gone(r, left[r])

    @pl.when(x < 3)
    def _():
        gone(4, left[4])


def shards(image_student, head_weight, text_student, image_teacher, text_teacher, logit_scales, logit_biases, loss_scale):
    vm = pltpu.VMEM
    scratch = [
        vm((2, 128, 768), bf16),
        vm((2, 128, 1152), bf16),
        vm((768, 768), bf16),
        vm((16, 768), bf16),
        vm((16, 1152), bf16),
        vm((8, 4, 16, 768), bf16),
        vm((4, 8, 16, 1152), bf16),
        vm((2, 128, 768), f32),
        vm((2, 128, 768), bf16),
        vm((2, 128, 1), f32),
        vm((2, 128, 1152), bf16),
        vm((8, 96, 256), bf16),
        vm((8, 16, 768), f32),
        vm((3, 8, 16, 768), bf16),
        vm((3, 8, 16, 768), bf16),
        vm((8, 16, 768), bf16),
        vm((7, 16, 768), bf16),
        vm((256, 768), f32),
        vm((6, 256, 128), f32),
        vm((3, 256, 128), f32),
        vm((3, 256, 128), f32),
        vm((3, 256, 128), bf16),
        vm((3, 256, 128), bf16),
        vm((8, 96, 128), f32),
        vm((8, 96, 128), bf16),
        vm((7, 96, 128), bf16),
        vm((4, 24, 128), f32),
        vm((7, 24, 128), f32),
        vm((6, 24, 128), f32),
        vm((1, 256), f32),
        vm((3, 8, 128), f32),
        vm((8, 128), f32),
        vm((3, 8, 128), f32),
        vm((2, 8, 128), f32),
        vm((ROOM, 8, 128), f32),
        pltpu.SMEM((2,), f32),
        pltpu.SMEM((2,), f32),
        pltpu.SMEM((1,), f32),
        pltpu.SemaphoreType.DMA((8,)),
        pltpu.SemaphoreType.DMA((5,)),
        pltpu.SemaphoreType.DMA((MESSAGES,)),
    ]
    hbm = pl.BlockSpec(memory_space=pltpu.HBM)
    vmem = pl.BlockSpec(memory_space=pltpu.VMEM)
    head, text, loss = pl.pallas_call(
        kernel,
        out_shape=(
            pltpu.VMEM((12, 768), f32),
            pltpu.VMEM((16, 768), f32),
            pltpu.VMEM((1, 128), f32),
        ),
        in_specs=[hbm] * 8,
        out_specs=(vmem, vmem, vmem),
        scratch_shapes=scratch,
        compiler_params=pltpu.CompilerParams(collective_id=0, has_side_effects=True, vmem_limit_bytes=60 * 1024 * 1024),
        name="distill",
    )(image_student, head_weight, text_student, image_teacher, text_teacher, logit_scales, logit_biases, loss_scale)
    return head, text, loss.reshape(128)


def solution(mesh):
    placed = (
        P("blk", None), P(), P(("blk", "txt"), None), P("blk", None), P(("blk", "txt"), None), P(), P(), P(),
    )
    return jax.shard_map(
        shards,
        mesh=mesh,
        in_specs=placed,
        out_specs=(P("blk", None), P(("blk", "txt"), None), P("blk")),
        check_vma=False,
    )
```

time: 76.6 us -> 64.9 us (0.85)
  local copies, waits for them, and re-layouts: 7.72 us -> 1.75 us
  Pallas kernels: 67.2 us -> 61.8 us
    unnamed x17 -> x3, local copies, waits for them, and re-layouts: 7.72 us -> 1.75 us
    pallas_call x1, Pallas kernels: 67.2 us -> 61.8 us  [shards(): pl.pallas_call(kernel, out_shape=(pltpu.VMEM((12, 768), f32), pltpu.VMEM(...]
where the time goes in v2:
time: 64.9 us; the launch traced here: 64.8 us
  Pallas kernels  61.8 us (95%)
  local copies, waits for them, and re-layouts  1.75 us (3%)
  between operations  1.29 us (2%)
    pallas_call x1, Pallas kernels, shards(): pl.pallas_call(kernel, out_shape=(pltpu.VMEM((12, 768), f32), pltpu.VMEM(...  61.8 us
    unnamed x3, local copies, waits for them, and re-layouts  1.75 us

profile of v2, /device:TPU:1, one launch (start us, length us, event | category | flops | bytes accessed | tf_op | source)
XLA Modules:
  0.0 64.8 jit_solution(9185772106024193515)
XLA Ops:
  1.3 61.8 %distill.1 = (f32[12,768]{1,0:T(8,128)S(1)}, f32[16,768]{1,0:T(8,128)S(1)}, f32[1,128]{1,0:T(1,128)S(1)}) custom-call(bf16[128,768]{1,0:T(8,128)(2,1)} %x_hbm.1, bf16[768,768]{1,0:T(8,128)(2,1)} %w_hbm.1, bf16[16,768]{1,0:T(8,128)(2,1)} %ts_hbm.1, bf16[128,1152]{1,0:T(8,128)(2,1)} %xt_hbm.1, bf16[16,1152]{1,0:T(8,128)(2,1)} %tt_hbm.1, f32[2]{0:T(128)} %scales_hbm.1, ...), custom_call_target="tpu_custom_call" | custom-call | tf_op jit(solution)/shard_map/distill/pallas_call | solution.py:408
  63.1 0.6 copy.14
  63.7 0.5 copy.16
  64.2 0.6 copy.15

commit v3 on v2

--- a/solution.py
+++ b/solution.py
@@ -13,9 +13,23 @@
 bf16 = jnp.bfloat16
 
 FLOW = {1: (1, 1), 2: (1, -1), 3: (2, 1), 4: (2, -1), 5: (3, 1), 6: (3, -1), 7: (4, 1)}
-NEXT = {1: 3, 2: 4, 3: 5, 4: 6, 5: 7}
+BEFORE = {1: 0, 2: 0, 3: 1, 4: 2, 5: 3, 6: 4, 7: 5}
 GROUPS = [(0, 1), (1, 2), (3, 2), (5, 2), (7, 1)]
 ZFLOW = {1: 1, 2: -1, 3: 2}
+ORDER = [
+    ("ty", 1), ("ty", 2), ("sz", 1), ("sz", 2), ("sz", 3), ("sy", 1, 0), ("sy", 2, 0), ("tz", 1, 0), ("tz", 2, 0),
+    ("images",), ("prepare", 0), ("prepare", 1), ("turn",),
+    ("ty", 3), ("ty", 4), ("sy", 1, 1), ("sy", 2, 1), ("sy", 3, 0), ("tz", 1, 1), ("sy", 4, 0), ("tz", 2, 1), ("tz", 3, 0),
+    ("sy", 1, 2), ("sy", 2, 2), ("ty", 5), ("sy", 5, 0), ("ty", 6), ("tz", 1, 2), ("tz", 2, 2), ("tz", 3, 1), ("sy", 6, 0),
+    ("tile", 0),
+    ("sy", 3, 1), ("sy", 3, 2), ("ty", 7), ("sy", 4, 1), ("sy", 4, 2), ("sy", 7, 0), ("tz", 1, 3), ("tz", 2, 3), ("tz", 3, 2),
+    ("sy", 5, 2),
+    ("tile", 1),
+    ("sy", 5, 1), ("tz", 1, 4), ("sy", 6, 1), ("tz", 2, 4), ("tz", 3, 3), ("sy", 6, 2), ("sy", 7, 2),
+    ("tile", 2),
+    ("tz", 3, 4), ("sy", 7, 1),
+    ("tile", 3),
+]
 
 
 def contract_last(a, b):
@@ -42,7 +56,7 @@
     x_hbm, w_hbm, ts_hbm, xt_hbm, tt_hbm, scales_hbm, biases_hbm, loss_scale_hbm,
     head_out, text_out, loss_out,
     xall, xtall, w, ts, tt, sb, tb, unit, low, rad, teach, xtp,
-    town, zs, zr, ysend, yr, grad, sfull, crecv, csum, sx, xr, hsum, hb, hr, zb, zrec, ag, lpart, lc, lx, lxr, lh,
+    town, zs, zr, ysend, yr, grad, csend, crecv, csum, sx, xr, hsum, hb, hr, zb, zrec, agsend, ag, lpart, lc, lx, lxr, lh,
     room, scales, biases, loss_scale, local_sem, send_sem, recv_sem,
 ):
     blk = lax.axis_index("blk")
@@ -122,37 +136,61 @@
         start, count = GROUPS[group]
         return tb.at[b, pl.ds(start, count)]
 
-    def send_s_y(pos_from, part):
-        targets = [(1, 1), (2, -1)] if pos_from == 0 else [(NEXT[pos_from], FLOW[pos_from][1])] if pos_from in NEXT else []
-        for pos, sign in targets:
-            send(("sy", pos, part), s_part(pos_from, part), s_part(pos, part), y_to[sign])
-
-    def send_t_y(pos_from):
-        targets = [(1, 1), (2, -1)] if pos_from == 0 else [(NEXT[pos_from], FLOW[pos_from][1])] if pos_from in NEXT else []
-        for pos, sign in targets:
-            send(("ty", pos), tb.at[0, pos_from], tb.at[0, pos], y_to[sign])
-
-    def send_t_z(group):
-        send(("tz", 1, group), t_group(0, group), t_group(1, group), z_to[1])
-        send(("tz", 2, group), t_group(0, group), t_group(2, group), z_to[-1])
-
-    send_t_y(0)
-    send(("sz", 1), sb.at[0, 0], sb.at[0, 1], z_to[1])
-    send(("sz", 1), sb.at[0, 0], sb.at[0, 2], z_to[-1])
-    send(("sz", 3), sb.at[0, 0], sb.at[0, 3], at(dz=2 * sgn))
-    send_s_y(0, 0)
-    send_t_z(0)
-    loads[2].wait()
-    loads[3].wait()
-    send("imgs", xall.at[c], xall.at[c], sibling)
-    send("imgt", xtall.at[c], xtall.at[c], sibling)
+    def gather_message(key):
+        kind = key[0]
+        if kind == "ty":
+            pos = key[1]
+            return [("ty", BEFORE[pos])], tb.at[0, BEFORE[pos]], tb.at[0, pos], y_to[FLOW[pos][1]]
+        if kind == "sy":
+            pos, part = key[1:]
+            parents = [("sy", BEFORE[pos], part)] if BEFORE[pos] else [[], [("sz", 1)], [("sz", 3)]][part]
+            return parents, s_part(BEFORE[pos], part), s_part(pos, part), y_to[FLOW[pos][1]]
+        if kind == "sz":
+            b = key[1]
+            return [], sb.at[0, 0], sb.at[0, b], at(dz=ZFLOW[b] * sgn)
+        b, group = key[1:]
+        start, count = GROUPS[group]
+        if b == 3:
+            return [("tz", 1, group)], t_group(1, group), t_group(3, group), z_to[1]
+        return [("ty", pos) for pos in range(start, start + count)], t_group(0, group), t_group(b, group), z_to[ZFLOW[b]]
+
+    waited = {("ty", 0)}
+
+    def need(key):
+        if key in waited:
+            return
+        waited.add(key)
+        kind = key[0]
+        if kind == "ty":
+            arrive(key, tb.at[0, key[1]])
+        elif kind == "sy":
+            arrive(key, s_part(key[1], key[2]))
+        elif kind == "sz":
+            arrive(key, s_part(0, 1) if key[1] == 1 else s_part(0, 2))
+        elif key[1] == 1:
+            arrive(key, t_group(1, key[2]))
+        else:
+            start, count = GROUPS[key[2]]
+            arrive(key, tb.at[pl.ds(2, 2), pl.ds(start, count)])
+
+    def pass_on(key):
+        parents, src, dst, device = gather_message(key)
+        for parent in parents:
+            need(parent)
+        if key[0] == "tz" and key[1] == 3:
+            key = ("tz", 2, key[2])
+        if key == ("sz", 2):
+            key = ("sz", 1)
+        send(key, src, dst, device)
 
     def prepare(k):
         projected = jnp.dot(xall[k], w[...], preferred_element_type=f32)
         radius = jnp.sqrt(jnp.sum(projected * projected, axis=1, keepdims=True) + epsilon)
         u = projected / radius
-        unit[k] = u
-        rad[k] = radius
+        here = pl.ds(128 * k, 128)
+        for j in range(6):
+            unit[j, here] = u[:, 128 * j : 128 * (j + 1)]
+        rad[here] = 1.0 / radius
         low[k] = u.astype(bf16)
         v = xtall[k].astype(f32)
         teach[k] = (v / jnp.sqrt(jnp.sum(v * v, axis=1, keepdims=True) + epsilon)).astype(bf16)
@@ -164,32 +202,15 @@
                 rows = [flat[zl * 192 + yy * 24 : zl * 192 + yy * 24 + 24] for zl in range(4)]
                 xtp[yy, :, 128 * k : 128 * (k + 1)] = jnp.concatenate(rows, axis=0).astype(bf16)
 
-    def hop(h):
-        for pos in range(1, 8):
-            if FLOW[pos][0] == h:
-                arrive(("ty", pos), tb.at[0, pos])
-                send_t_y(pos)
-        if h <= 4:
-            send_t_z(h)
-        if h == 1:
-            arrive(("sz", 1), s_part(0, 1))
-            send_s_y(0, 1)
-        if h == 2:
-            arrive(("sz", 3), sb.at[0, 3])
-            send_s_y(0, 2)
-        for part in range(3):
-            for pos in range(1, 8):
-                if FLOW[pos][0] + part == h:
-                    arrive(("sy", pos, part), s_part(pos, part))
-                    send_s_y(pos, part)
-        if 0 <= h - 1 <= 4:
-            group = h - 1
-            arrive(("tz", 1, group), t_group(1, group))
-            send(("tz", 2, group), t_group(1, group), t_group(3, group), z_to[1])
-
     def tile(group):
         start, count = GROUPS[group]
-        arrive(("tz", 2, group), tb.at[pl.ds(2, 2), pl.ds(start, count)])
+        for pos in range(start, start + count):
+            need(("ty", pos))
+            for part in range(3):
+                if pos:
+                    need(("sy", pos, part))
+        for key in [("sz", 1), ("sz", 3), ("tz", 1, group), ("tz", 2, group)]:
+            need(key)
         n = count * 64
         rows = sb[start : start + count].reshape(n, 768)
         teach_rows = jnp.concatenate([tb[:, p].reshape(64, 1152) for p in range(start, start + count)], axis=0)
@@ -206,11 +227,16 @@
         gradient = contract_first(errors, rows)
         if group == 0:
             lpart[...] = part
-            grad[...] = gradient
         else:
             lpart[...] += part
-            grad[...] += gradient
-        term = jnp.dot(errors, low_all, preferred_element_type=f32).reshape(count, 4, 16, 768)
+        for j in range(6):
+            columns = gradient[:, 128 * j : 128 * (j + 1)]
+            grad[j] = columns if group == 0 else grad[j] + columns
+        return errors
+
+    def terms(group, errors):
+        start, count = GROUPS[group]
+        term = jnp.dot(errors, low[...].reshape(256, 768), preferred_element_type=f32).reshape(count, 4, 16, 768)
         town[start : start + count] = term[:, 0]
         for b in (1, 2, 3):
             zs[b - 1, start : start + count] = term[:, b].astype(bf16)
@@ -231,51 +257,65 @@
         steps, sign = FLOW[pos]
         send("gy", ysend.at[pos], yr.at[pos - 1], at(dy=-steps * sign * sgn))
 
-    for copy in loads[4:]:
-        copy.wait()
-    hop(1)
-    arrive("imgs", xall.at[1 - c])
-    arrive("imgt", xtall.at[1 - c])
-    prepare(0)
-    hop(2)
-    prepare(1)
-    hop(3)
-    tile(0)
-    hop(4)
-    tile(1)
-    hop(5)
-    tile(2)
-    turn()
-    tile(3)
-    hop(6)
-    tile(4)
+    for action in ORDER:
+        kind = action[0]
+        if kind == "images":
+            loads[2].wait()
+            loads[3].wait()
+            send("imgs", xall.at[c], xall.at[c], sibling)
+            send("imgt", xtall.at[c], xtall.at[c], sibling)
+            for copy in loads[4:]:
+                copy.wait()
+        elif kind == "prepare":
+            if action[1] == 1:
+                arrive("imgs", xall.at[1 - c])
+                arrive("imgt", xtall.at[1 - c])
+            prepare(c if action[1] == 0 else 1 - c)
+        elif kind == "turn":
+            turn()
+        elif kind == "tile":
+            terms(action[1], tile(action[1]))
+        else:
+            pass_on(action)
+    last_errors = tile(4)
 
     factor = loss_scale[0] * scales[0] / 8192.0
-    g = grad[...] * factor
-    u = unit[...].reshape(256, 768)
-    step = (g - u * jnp.sum(g * u, axis=1, keepdims=True)) / rad[...].reshape(256, 1)
-    for j in range(6):
-        sfull[j] = step[:, 128 * j : 128 * (j + 1)]
+    radial = grad[0] * unit[0]
+    for j in range(1, 6):
+        radial = radial + grad[j] * unit[j]
+    radial = jnp.sum(radial, axis=1, keepdims=True)
+    over = rad[...] * factor
+
+    def step(j):
+        return (grad[j] - unit[j] * radial) * over
+
+    for j in range(3):
+        csend[j] = step(3 * (1 - c) + j)
+        send(("cs", j), csend.at[j], crecv.at[j], sibling)
+    for j in range(3):
+        csum[j] = step(3 * c + j)
     for k in range(2):
         lc[k] = jnp.broadcast_to(lpart[:, 128 * k : 128 * (k + 1)], (8, 128))
-    send("cs", sfull.at[pl.ds(3 * (1 - c), 3)], crecv, sibling)
     send("cl", lc.at[1 - c], lc.at[2], sibling)
+
+    for j in range(3):
+        arrive(("cs", j), crecv.at[j])
+        total = csum[j] + crecv[j]
+
+        @pl.when(x == j)
+        def _():
+            csum[j] = total
+
+        @pl.when(x != j)
+        def _():
+            sx[j] = total.astype(bf16)
+            send("xs", sx.at[j], xr.at[lax.rem(j - x + 4, 4) - 1], at(dx=j - x), lane=1 + j)
+
+    terms(4, last_errors)
     back_z()
-
-    arrive("cs", crecv)
-    total = sfull[pl.ds(3 * c, 3)] + crecv[...]
-    csum[...] = total
-    sx[...] = total.astype(bf16)
-    for r in (1, 2, 3):
-        xto = lax.rem(x + r, 4)
-
-        @pl.when(xto < 3)
-        def _():
-            send("xs", sx.at[lax.rem(xto, 3)], xr.at[r - 1], at(dx=r), lane=r)
-
     arrive("cl", lc.at[2])
     lx[...] = lc[c] + lc[2]
-    for r in (1, 2, 3):
+    for r in (2, 1, 3):
         send("xl", lx, lxr.at[r - 1], at(dx=r))
 
     @pl.when(x < 3)
@@ -283,13 +323,17 @@
         arrive("xs", xr)
         s = csum[x] + xr[0].astype(f32) + xr[1].astype(f32) + xr[2].astype(f32)
         high = s.astype(bf16)
-        rest = (s - high.astype(f32)).astype(bf16)
-        both = jnp.dot(xtp[...].reshape(768, 256), jnp.concatenate([high, rest], axis=1), preferred_element_type=f32)
-        h = (both[:, :128] + both[:, 128:]).reshape(8, 96, 128)
-        hsum[...] = h
-        hb[...] = h.astype(bf16)
-        for r in range(1, 8):
-            send("hy", hb.at[lax.rem(y + r, 8)], hr.at[r - 1], at(dy=r), lane=4)
+        both = jnp.concatenate([high, (s - high.astype(f32)).astype(bf16)], axis=1)
+        for half in ((4, 3, 5, 2), (6, 1, 7, 0)):
+            turned = jnp.concatenate([xtp[lax.rem(y + r, 8)] for r in half], axis=0)
+            product = jnp.dot(turned, both, preferred_element_type=f32)
+            h = (product[:, :128] + product[:, 128:]).reshape(4, 96, 128)
+            for place, r in enumerate(half):
+                if r == 0:
+                    hsum[...] = h[place]
+                else:
+                    hb[r - 1] = h[place].astype(bf16)
+                    send("hy", hb.at[r - 1], hr.at[r - 1], at(dy=r), lane=4)
 
     arrive("xl", lxr)
     lh[0] = lx[...] + lxr[0] + lxr[1] + lxr[2]
@@ -299,11 +343,11 @@
     @pl.when(x < 3)
     def _():
         arrive("hy", hr)
-        total = hsum[y]
+        total = hsum[...]
         for r in range(1, 8):
             total = total + hr[r - 1].astype(f32)
         zb[...] = total.reshape(4, 24, 128)
-        for r in range(1, 8):
+        for r in (4, 3, 5, 2, 6, 1, 7):
             send("hz", zb.at[lax.rem(z + r, 4)], zrec.at[r - 1], at(dz=r), lane=4)
 
     for pos in range(7, 0, -1):
@@ -319,11 +363,13 @@
         total = zb[lax.rem(z, 4)]
         for r in range(1, 8):
             total = total + zrec[r - 1]
-        ag[mine] = total
-        send("ag", ag.at[mine], ag.at[mine], sibling, lane=4)
-        for r in (1, 2, 3):
+        agsend[0] = total[0:16]
+        agsend[1] = total[8:24]
+        ag[mine] = agsend[c]
+        for r in (2, 1, 3):
             for k in (0, 1):
-                send("ag", ag.at[mine], ag.at[mine], at(dx=r, core=c if k == 0 else 1 - c), lane=4)
+                send("ag", agsend.at[k], ag.at[mine], at(dx=r, core=k), lane=4)
+        send("ag", agsend.at[1 - c], ag.at[mine], sibling, lane=4)
 
     arrive("gy", yr)
     tg = town[0]
@@ -344,14 +390,14 @@
         arrive("ag", ag)
 
     for j in range(6):
-        head_out[:, 128 * j : 128 * (j + 1)] = jnp.where(c == 0, ag[j, 0:12], ag[j, 12:24])
+        head_out[:, 128 * j : 128 * (j + 1)] = jnp.where(c == 0, ag[j, 0:12], ag[j, 4:16])
 
     gone(0, left[0])
-    for r in (1, 2, 3):
-
-        @pl.when(lax.rem(x + r, 4) < 3)
+    for j in range(3):
+
+        @pl.when(x != j)
         def _():
-            gone(r, left[r])
+            gone(1 + j, left[1 + j])
 
     @pl.when(x < 3)
     def _():
@@ -368,9 +414,9 @@
         vm((16, 1152), bf16),
         vm((8, 4, 16, 768), bf16),
         vm((4, 8, 16, 1152), bf16),
-        vm((2, 128, 768), f32),
+        vm((6, 256, 128), f32),
         vm((2, 128, 768), bf16),
-        vm((2, 128, 1), f32),
+        vm((256, 1), f32),
         vm((2, 128, 1152), bf16),
         vm((8, 96, 256), bf16),
         vm((8, 16, 768), f32),
@@ -378,18 +424,19 @@
         vm((3, 8, 16, 768), bf16),
         vm((8, 16, 768), bf16),
         vm((7, 16, 768), bf16),
-        vm((256, 768), f32),
         vm((6, 256, 128), f32),
+        vm((3, 256, 128), f32),
         vm((3, 256, 128), f32),
         vm((3, 256, 128), f32),
         vm((3, 256, 128), bf16),
         vm((3, 256, 128), bf16),
-        vm((8, 96, 128), f32),
-        vm((8, 96, 128), bf16),
+        vm((96, 128), f32),
+        vm((7, 96, 128), bf16),
         vm((7, 96, 128), bf16),
         vm((4, 24, 128), f32),
         vm((7, 24, 128), f32),
-        vm((6, 24, 128), f32),
+        vm((2, 16, 128), f32),
+        vm((6, 16, 128), f32),
         vm((1, 256), f32),
         vm((3, 8, 128), f32),
         vm((8, 128), f32),

time: 64.9 us -> 61 us (0.940)
  Pallas kernels: 61.8 us -> 57.8 us
    pallas_call x1, Pallas kernels: 61.8 us -> 57.8 us  [shards(): pl.pallas_call(kernel, out_shape=(pltpu.VMEM((12, 768), f32), pltpu.VMEM(...]
where the time goes in v3:
time: 61 us; the launch traced here: 60.8 us
  Pallas kernels  57.8 us (95%)
  local copies, waits for them, and re-layouts  1.75 us (3%)
  between operations  1.29 us (2%)
    pallas_call x1, Pallas kernels, shards(): pl.pallas_call(kernel, out_shape=(pltpu.VMEM((12, 768), f32), pltpu.VMEM(...  57.8 us
    unnamed x3, local copies, waits for them, and re-layouts  1.75 us

profile of v3, /device:TPU:1, one launch (start us, length us, event | category | flops | bytes accessed | tf_op | source)
XLA Modules:
  0.0 60.8 jit_solution(12814867094428316354)
XLA Ops:
  1.3 57.8 %distill.1 = (f32[12,768]{1,0:T(8,128)S(1)}, f32[16,768]{1,0:T(8,128)S(1)}, f32[1,128]{1,0:T(1,128)S(1)}) custom-call(bf16[128,768]{1,0:T(8,128)(2,1)} %x_hbm.1, bf16[768,768]{1,0:T(8,128)(2,1)} %w_hbm.1, bf16[16,768]{1,0:T(8,128)(2,1)} %ts_hbm.1, bf16[128,1152]{1,0:T(8,128)(2,1)} %xt_hbm.1, bf16[16,1152]{1,0:T(8,128)(2,1)} %tt_hbm.1, f32[2]{0:T(128)} %scales_hbm.1, ...), custom_call_target="tpu_custom_call" | custom-call | tf_op jit(solution)/shard_map/distill/pallas_call | solution.py:455
  59.1 0.6 %copy.14 = f32[12,768]{1,0:T(8,128)} copy(f32[12,768]{1,0:T(8,128)S(1)} %get-tuple-element.9) | data formatting | bytes 73728
  59.7 0.5 copy.16
  60.2 0.6 %copy.15 = f32[16,768]{1,0:T(8,128)} copy(f32[16,768]{1,0:T(8,128)S(1)} %get-tuple-element.10) | data formatting | bytes 98304

commit v4 on v3

--- a/solution.py
+++ b/solution.py
@@ -13,22 +13,21 @@
 bf16 = jnp.bfloat16
 
 FLOW = {1: (1, 1), 2: (1, -1), 3: (2, 1), 4: (2, -1), 5: (3, 1), 6: (3, -1), 7: (4, 1)}
-BEFORE = {1: 0, 2: 0, 3: 1, 4: 2, 5: 3, 6: 4, 7: 5}
+T_TREE = {1: (0, 1), 2: (0, 1), 3: (0, 2), 4: (0, 2), 5: (1, 2), 6: (4, 1), 7: (5, 1)}
+S_TREES = [
+    {1: (0, 1), 2: (0, 1), 3: (1, 1), 4: (2, 1), 5: (3, 1), 6: (4, 1), 7: (3, 2)},
+    {1: (0, 1), 2: (0, 1), 3: (0, 2), 4: (0, 2), 5: (1, 2), 6: (2, 2), 7: (3, 2)},
+]
+LONG = (0, 3)
 GROUPS = [(0, 1), (1, 2), (3, 2), (5, 2), (7, 1)]
 ZFLOW = {1: 1, 2: -1, 3: 2}
 ORDER = [
-    ("ty", 1), ("ty", 2), ("sz", 1), ("sz", 2), ("sz", 3), ("sy", 1, 0), ("sy", 2, 0), ("tz", 1, 0), ("tz", 2, 0),
-    ("images",), ("prepare", 0), ("prepare", 1), ("turn",),
-    ("ty", 3), ("ty", 4), ("sy", 1, 1), ("sy", 2, 1), ("sy", 3, 0), ("tz", 1, 1), ("sy", 4, 0), ("tz", 2, 1), ("tz", 3, 0),
-    ("sy", 1, 2), ("sy", 2, 2), ("ty", 5), ("sy", 5, 0), ("ty", 6), ("tz", 1, 2), ("tz", 2, 2), ("tz", 3, 1), ("sy", 6, 0),
-    ("tile", 0),
-    ("sy", 3, 1), ("sy", 3, 2), ("ty", 7), ("sy", 4, 1), ("sy", 4, 2), ("sy", 7, 0), ("tz", 1, 3), ("tz", 2, 3), ("tz", 3, 2),
-    ("sy", 5, 2),
-    ("tile", 1),
-    ("sy", 5, 1), ("tz", 1, 4), ("sy", 6, 1), ("tz", 2, 4), ("tz", 3, 3), ("sy", 6, 2), ("sy", 7, 2),
-    ("tile", 2),
-    ("tz", 3, 4), ("sy", 7, 1),
-    ("tile", 3),
+    ("ty", 1), ("sz", 1), ("sz", 2), ("ty", 4), ("ty", 3), ("ty", 2), ("sz", 3), ("tz", 3, 0), ("tz", 1, 0), ("tz", 2, 0),
+    ("images",), ("prepare", 0), ("prepare", 1), ("ty", 5), ("turn",), ("sy", 1, 0), ("sy", 2, 0), ("tz", 1, 1),
+    ("tz", 2, 1), ("ty", 6), ("tz", 1, 2), ("sy", 3, 1), ("sy", 1, 1), ("sy", 2, 1), ("tz", 2, 2), ("sy", 4, 1), ("tile", 0),
+    ("ty", 7), ("sy", 3, 0), ("sy", 4, 0), ("tz", 3, 1), ("tz", 3, 3), ("tz", 1, 3), ("tz", 2, 3), ("sy", 5, 1),
+    ("sy", 6, 1), ("tz", 3, 2), ("tz", 1, 4), ("sy", 7, 1), ("tz", 2, 4), ("sy", 7, 0), ("sy", 5, 0), ("sy", 6, 0),
+    ("tile", 1), ("tz", 3, 4), ("tile", 2), ("tile", 3),
 ]
 
 
@@ -56,7 +55,7 @@
     x_hbm, w_hbm, ts_hbm, xt_hbm, tt_hbm, scales_hbm, biases_hbm, loss_scale_hbm,
     head_out, text_out, loss_out,
     xall, xtall, w, ts, tt, sb, tb, unit, low, rad, teach, xtp,
-    town, zs, zr, ysend, yr, grad, csend, crecv, csum, sx, xr, hsum, hb, hr, zb, zrec, agsend, ag, lpart, lc, lx, lxr, lh,
+    kept, town, zs, zr, ysend, yr, grad, csend, crecv, csum, sx, xr, hsum, hb, hr, zb, zrec, agsend, ag, lpart, lc, lx, lxr, lh,
     room, scales, biases, loss_scale, local_sem, send_sem, recv_sem,
 ):
     blk = lax.axis_index("blk")
@@ -72,13 +71,6 @@
         yy = lax.rem(y + dy + 16, 8)
         zz = lax.rem(z + dz + 16, 8)
         return {"blk": (lax.rem(zz, 4) * 8 + yy) * 2 + core, "txt": (zz // 4) * 4 + xx}
-
-    barrier = pltpu.get_barrier_semaphore()
-    partners = [at(core=1 - c)]
-    partners += [at(dy=1), at(dy=-1), at(dz=1), at(dz=-1)]
-    partners += [at(dz=-2 * sgn)] + [at(dx=r) for r in (1, 2, 3)]
-    for partner in partners:
-        pl.semaphore_signal(barrier, inc=1, device_id=partner, device_id_type=MESH)
 
     loads = [
         pltpu.make_async_copy(ts_hbm, ts, local_sem.at[0]),
@@ -90,7 +82,18 @@
         pltpu.make_async_copy(biases_hbm, biases, local_sem.at[6]),
         pltpu.make_async_copy(loss_scale_hbm, loss_scale, local_sem.at[7]),
     ]
-    for copy in loads:
+    for copy in loads[:2]:
+        copy.start()
+
+    barrier = pltpu.get_barrier_semaphore()
+    partners = [at(core=1 - c)]
+    partners += [at(dy=1), at(dy=-1), at(dz=1), at(dz=-1)]
+    partners += [at(dy=-k * sgn) for k in (-2, 2)]
+    partners += [at(dz=-2 * sgn)] + [at(dx=r) for r in (1, 2, 3)]
+    for partner in partners:
+        pl.semaphore_signal(barrier, inc=1, device_id=partner, device_id_type=MESH)
+
+    for copy in loads[2:]:
         copy.start()
 
     tags = Tags()
@@ -126,11 +129,10 @@
 
     pl.semaphore_wait(barrier, len(partners))
 
-    y_to = {1: at(dy=sgn), -1: at(dy=-sgn)}
     z_to = {1: at(dz=sgn), -1: at(dz=-sgn)}
 
     def s_part(pos, part):
-        return sb.at[pos, pl.ds(0, 1)] if part == 0 else sb.at[pos, pl.ds(1, 2)] if part == 1 else sb.at[pos, pl.ds(3, 1)]
+        return sb.at[pos, pl.ds(0, 3)] if part == 0 else sb.at[pos, pl.ds(3, 1)]
 
     def t_group(b, group):
         start, count = GROUPS[group]
@@ -140,19 +142,21 @@
         kind = key[0]
         if kind == "ty":
             pos = key[1]
-            return [("ty", BEFORE[pos])], tb.at[0, BEFORE[pos]], tb.at[0, pos], y_to[FLOW[pos][1]]
+            before, far = T_TREE[pos]
+            return [("ty", before)], tb.at[0, before], tb.at[0, pos], at(dy=FLOW[pos][1] * far * sgn)
         if kind == "sy":
             pos, part = key[1:]
-            parents = [("sy", BEFORE[pos], part)] if BEFORE[pos] else [[], [("sz", 1)], [("sz", 3)]][part]
-            return parents, s_part(BEFORE[pos], part), s_part(pos, part), y_to[FLOW[pos][1]]
+            before, far = S_TREES[part][pos]
+            parents = [("sy", before, part)] if before else [[("sz", 1)], [("sz", 3)]][part]
+            return parents, s_part(before, part), s_part(pos, part), at(dy=FLOW[pos][1] * far * sgn)
         if kind == "sz":
             b = key[1]
             return [], sb.at[0, 0], sb.at[0, b], at(dz=ZFLOW[b] * sgn)
         b, group = key[1:]
         start, count = GROUPS[group]
-        if b == 3:
+        if b == 3 and group not in LONG:
             return [("tz", 1, group)], t_group(1, group), t_group(3, group), z_to[1]
-        return [("ty", pos) for pos in range(start, start + count)], t_group(0, group), t_group(b, group), z_to[ZFLOW[b]]
+        return [("ty", pos) for pos in range(start, start + count)], t_group(0, group), t_group(b, group), at(dz=ZFLOW[b] * sgn)
 
     waited = {("ty", 0)}
 
@@ -166,7 +170,7 @@
         elif kind == "sy":
             arrive(key, s_part(key[1], key[2]))
         elif kind == "sz":
-            arrive(key, s_part(0, 1) if key[1] == 1 else s_part(0, 2))
+            arrive(key, sb.at[0, pl.ds(1, 2)] if key[1] == 1 else s_part(0, 1))
         elif key[1] == 1:
             arrive(key, t_group(1, key[2]))
         else:
@@ -206,7 +210,7 @@
         start, count = GROUPS[group]
         for pos in range(start, start + count):
             need(("ty", pos))
-            for part in range(3):
+            for part in range(2):
                 if pos:
                     need(("sy", pos, part))
         for key in [("sz", 1), ("sz", 3), ("tz", 1, group), ("tz", 2, group)]:
@@ -232,14 +236,14 @@
         for j in range(6):
             columns = gradient[:, 128 * j : 128 * (j + 1)]
             grad[j] = columns if group == 0 else grad[j] + columns
-        return errors
-
-    def terms(group, errors):
-        start, count = GROUPS[group]
-        term = jnp.dot(errors, low[...].reshape(256, 768), preferred_element_type=f32).reshape(count, 4, 16, 768)
-        town[start : start + count] = term[:, 0]
+        kept[start : start + count] = errors.reshape(count, 64, 256)
+
+    def terms():
+        term = jnp.dot(kept[...].reshape(512, 256), low[...].reshape(256, 768), preferred_element_type=f32)
+        term = term.reshape(8, 4, 16, 768)
+        town[...] = term[:, 0]
         for b in (1, 2, 3):
-            zs[b - 1, start : start + count] = term[:, b].astype(bf16)
+            zs[b - 1] = term[:, b].astype(bf16)
 
     def back_z():
         for b in (3, 1, 2):
@@ -274,10 +278,10 @@
         elif kind == "turn":
             turn()
         elif kind == "tile":
-            terms(action[1], tile(action[1]))
+            tile(action[1])
         else:
             pass_on(action)
-    last_errors = tile(4)
+    tile(4)
 
     factor = loss_scale[0] * scales[0] / 8192.0
     radial = grad[0] * unit[0]
@@ -290,7 +294,7 @@
         return (grad[j] - unit[j] * radial) * over
 
     for j in range(3):
-        csend[j] = step(3 * (1 - c) + j)
+        csend[j] = step(3 * (1 - c) + j).astype(bf16)
         send(("cs", j), csend.at[j], crecv.at[j], sibling)
     for j in range(3):
         csum[j] = step(3 * c + j)
@@ -300,7 +304,7 @@
 
     for j in range(3):
         arrive(("cs", j), crecv.at[j])
-        total = csum[j] + crecv[j]
+        total = csum[j] + crecv[j].astype(f32)
 
         @pl.when(x == j)
         def _():
@@ -311,7 +315,7 @@
             sx[j] = total.astype(bf16)
             send("xs", sx.at[j], xr.at[lax.rem(j - x + 4, 4) - 1], at(dx=j - x), lane=1 + j)
 
-    terms(4, last_errors)
+    terms()
     back_z()
     arrive("cl", lc.at[2])
     lx[...] = lc[c] + lc[2]
@@ -419,14 +423,15 @@
         vm((256, 1), f32),
         vm((2, 128, 1152), bf16),
         vm((8, 96, 256), bf16),
+        vm((8, 64, 256), bf16),
         vm((8, 16, 768), f32),
         vm((3, 8, 16, 768), bf16),
         vm((3, 8, 16, 768), bf16),
         vm((8, 16, 768), bf16),
         vm((7, 16, 768), bf16),
         vm((6, 256, 128), f32),
-        vm((3, 256, 128), f32),
-        vm((3, 256, 128), f32),
+        vm((3, 256, 128), bf16),
+        vm((3, 256, 128), bf16),
         vm((3, 256, 128), f32),
         vm((3, 256, 128), bf16),
         vm((3, 256, 128), bf16),

time: 61 us -> 59.2 us (0.970)
  Pallas kernels: 57.8 us -> 56 us
    pallas_call x1, Pallas kernels: 57.8 us -> 56 us  [shards(): pl.pallas_call(kernel, out_shape=(pltpu.VMEM((12, 768), f32), pltpu.VMEM(...]
where the time goes in v4:
time: 59.2 us; the launch traced here: 59 us
  Pallas kernels  56 us (95%)
  local copies, waits for them, and re-layouts  1.75 us (3%)
  between operations  1.29 us (2%)
    pallas_call x1, Pallas kernels, shards(): pl.pallas_call(kernel, out_shape=(pltpu.VMEM((12, 768), f32), pltpu.VMEM(...  56 us
    unnamed x3, local copies, waits for them, and re-layouts  1.75 us

profile of v4, /device:TPU:1, one launch (start us, length us, event | category | flops | bytes accessed | tf_op | source)
XLA Modules:
  0.0 59.0 jit_solution(8293469069489367861)
XLA Ops:
  1.3 56.0 %distill.1 = (f32[12,768]{1,0:T(8,128)S(1)}, f32[16,768]{1,0:T(8,128)S(1)}, f32[1,128]{1,0:T(1,128)S(1)}) custom-call(bf16[128,768]{1,0:T(8,128)(2,1)} %x_hbm.1, bf16[768,768]{1,0:T(8,128)(2,1)} %w_hbm.1, bf16[16,768]{1,0:T(8,128)(2,1)} %ts_hbm.1, bf16[128,1152]{1,0:T(8,128)(2,1)} %xt_hbm.1, bf16[16,1152]{1,0:T(8,128)(2,1)} %tt_hbm.1, f32[2]{0:T(128)} %scales_hbm.1, ...), custom_call_target="tpu_custom_call" | custom-call | tf_op jit(solution)/shard_map/distill/pallas_call | solution.py:460
  57.3 0.6 %copy.14 = f32[12,768]{1,0:T(8,128)} copy(f32[12,768]{1,0:T(8,128)S(1)} %get-tuple-element.9) | data formatting | bytes 73728
  57.9 0.5 copy.16
  58.4 0.6 %copy.15 = f32[16,768]{1,0:T(8,128)} copy(f32[16,768]{1,0:T(8,128)S(1)} %get-tuple-element.10) | data formatting | bytes 98304

commit v5 on v4

--- a/solution.py
+++ b/solution.py
@@ -47,7 +47,7 @@
         return self.index.setdefault(key, len(self.index))
 
 
-MESSAGES = 56
+MESSAGES = 47
 ROOM = 2048
 
 
@@ -82,18 +82,13 @@
         pltpu.make_async_copy(biases_hbm, biases, local_sem.at[6]),
         pltpu.make_async_copy(loss_scale_hbm, loss_scale, local_sem.at[7]),
     ]
-    for copy in loads[:2]:
-        copy.start()
-
     barrier = pltpu.get_barrier_semaphore()
-    partners = [at(core=1 - c)]
-    partners += [at(dy=1), at(dy=-1), at(dz=1), at(dz=-1)]
-    partners += [at(dy=-k * sgn) for k in (-2, 2)]
-    partners += [at(dz=-2 * sgn)] + [at(dx=r) for r in (1, 2, 3)]
+    partners = [at(dx=2), at(dy=2), at(dy=-2), at(dz=-2 * sgn)]
+    partners += [at(dx=1), at(dx=3), at(dy=1), at(dy=-1), at(dz=1), at(dz=-1), at(core=1 - c)]
     for partner in partners:
         pl.semaphore_signal(barrier, inc=1, device_id=partner, device_id_type=MESH)
 
-    for copy in loads[2:]:
+    for copy in loads:
         copy.start()
 
     tags = Tags()

time: 59.2 us -> 59.2 us (level)
  no operation moved by 1% of the time
where the time goes in v5:
time: 59.2 us; the launch traced here: 59.1 us
  Pallas kernels  56 us (95%)
  local copies, waits for them, and re-layouts  1.75 us (3%)
  between operations  1.29 us (2%)
    pallas_call x1, Pallas kernels, shards(): pl.pallas_call(kernel, out_shape=(pltpu.VMEM((12, 768), f32), pltpu.VMEM(...  56 us
    unnamed x3, local copies, waits for them, and re-layouts  1.75 us

profile of v5, /device:TPU:1, one launch (start us, length us, event | category | flops | bytes accessed | tf_op | source)
XLA Modules:
  0.0 59.1 jit_solution(3888411792822563335)
XLA Ops:
  1.3 56.0 %distill.1 = (f32[12,768]{1,0:T(8,128)S(1)}, f32[16,768]{1,0:T(8,128)S(1)}, f32[1,128]{1,0:T(1,128)S(1)}) custom-call(bf16[128,768]{1,0:T(8,128)(2,1)} %x_hbm.1, bf16[768,768]{1,0:T(8,128)(2,1)} %w_hbm.1, bf16[16,768]{1,0:T(8,128)(2,1)} %ts_hbm.1, bf16[128,1152]{1,0:T(8,128)(2,1)} %xt_hbm.1, bf16[16,1152]{1,0:T(8,128)(2,1)} %tt_hbm.1, f32[2]{0:T(128)} %scales_hbm.1, ...), custom_call_target="tpu_custom_call" | custom-call | tf_op jit(solution)/shard_map/distill/pallas_call | solution.py:455
  57.3 0.6 %copy.14 = f32[12,768]{1,0:T(8,128)} copy(f32[12,768]{1,0:T(8,128)S(1)} %get-tuple-element.9) | data formatting | bytes 73728
  57.9 0.5 copy.16
  58.5 0.6 %copy.15 = f32[16,768]{1,0:T(8,128)} copy(f32[16,768]{1,0:T(8,128)S(1)} %get-tuple-element.10) | data formatting | bytes 98304

commit v6 on v5

--- a/solution.py
+++ b/solution.py
@@ -55,7 +55,7 @@
     x_hbm, w_hbm, ts_hbm, xt_hbm, tt_hbm, scales_hbm, biases_hbm, loss_scale_hbm,
     head_out, text_out, loss_out,
     xall, xtall, w, ts, tt, sb, tb, unit, low, rad, teach, xtp,
-    kept, town, zs, zr, ysend, yr, grad, csend, crecv, csum, sx, xr, hsum, hb, hr, zb, zrec, agsend, ag, lpart, lc, lx, lxr, lh,
+    kept, town, zs, zr, ysend, yr, grad, csum, sx, xr, hsum, hb, hr, zb, zrec, agsend, ag, lpart, lc, lx, lxr, lh,
     room, scales, biases, loss_scale, local_sem, send_sem, recv_sem,
 ):
     blk = lax.axis_index("blk")
@@ -85,6 +85,7 @@
     barrier = pltpu.get_barrier_semaphore()
     partners = [at(dx=2), at(dy=2), at(dy=-2), at(dz=-2 * sgn)]
     partners += [at(dx=1), at(dx=3), at(dy=1), at(dy=-1), at(dz=1), at(dz=-1), at(core=1 - c)]
+    partners += [at(dx=r, core=1 - c) for r in (2, 1, 3)]
     for partner in partners:
         pl.semaphore_signal(barrier, inc=1, device_id=partner, device_id_type=MESH)
 
@@ -288,27 +289,28 @@
     def step(j):
         return (grad[j] - unit[j] * radial) * over
 
-    for j in range(3):
-        csend[j] = step(3 * (1 - c) + j).astype(bf16)
-        send(("cs", j), csend.at[j], crecv.at[j], sibling)
-    for j in range(3):
-        csum[j] = step(3 * c + j)
+    for other in (1, 0):
+        for j in (0, 1, 2):
+            core = 1 - c if other else c
+            columns = step(3 * core + j)
+            slot = lax.rem(j - x + 4, 4) * 2 + other - 1
+            if other:
+                sx[j, 1] = columns.astype(bf16)
+                send("xs", sx.at[j, 1], xr.at[slot], at(dx=j - x, core=core))
+            else:
+
+                @pl.when(x == j)
+                def _():
+                    csum[...] = columns
+
+                @pl.when(x != j)
+                def _():
+                    sx[j, 0] = columns.astype(bf16)
+                    send("xs", sx.at[j, 0], xr.at[slot], at(dx=j - x), lane=1 + j)
+
     for k in range(2):
         lc[k] = jnp.broadcast_to(lpart[:, 128 * k : 128 * (k + 1)], (8, 128))
     send("cl", lc.at[1 - c], lc.at[2], sibling)
-
-    for j in range(3):
-        arrive(("cs", j), crecv.at[j])
-        total = csum[j] + crecv[j].astype(f32)
-
-        @pl.when(x == j)
-        def _():
-            csum[j] = total
-
-        @pl.when(x != j)
-        def _():
-            sx[j] = total.astype(bf16)
-            send("xs", sx.at[j], xr.at[lax.rem(j - x + 4, 4) - 1], at(dx=j - x), lane=1 + j)
 
     terms()
     back_z()
@@ -320,7 +322,9 @@
     @pl.when(x < 3)
     def _():
         arrive("xs", xr)
-        s = csum[x] + xr[0].astype(f32) + xr[1].astype(f32) + xr[2].astype(f32)
+        s = csum[...]
+        for i in range(7):
+            s = s + xr[i].astype(f32)
         high = s.astype(bf16)
         both = jnp.concatenate([high, (s - high.astype(f32)).astype(bf16)], axis=1)
         for half in ((4, 3, 5, 2), (6, 1, 7, 0)):
@@ -425,11 +429,9 @@
         vm((8, 16, 768), bf16),
         vm((7, 16, 768), bf16),
         vm((6, 256, 128), f32),
-        vm((3, 256, 128), bf16),
-        vm((3, 256, 128), bf16),
-        vm((3, 256, 128), f32),
-        vm((3, 256, 128), bf16),
-        vm((3, 256, 128), bf16),
+        vm((256, 128), f32),
+        vm((3, 2, 256, 128), bf16),
+        vm((7, 256, 128), bf16),
         vm((96, 128), f32),
         vm((7, 96, 128), bf16),
         vm((7, 96, 128), bf16),

time: 59.2 us -> 59.2 us (level)
  no operation moved by 1% of the time
where the time goes in v6:
time: 59.2 us; the launch traced here: 59.1 us
  Pallas kernels  56 us (95%)
  local copies, waits for them, and re-layouts  1.75 us (3%)
  between operations  1.29 us (2%)
    pallas_call x1, Pallas kernels, shards(): pl.pallas_call(kernel, out_shape=(pltpu.VMEM((12, 768), f32), pltpu.VMEM(...  56 us
    unnamed x3, local copies, waits for them, and re-layouts  1.75 us

profile of v6, /device:TPU:1, one launch (start us, length us, event | category | flops | bytes accessed | tf_op | source)
XLA Modules:
  0.0 59.1 jit_solution(3050171620555231803)
XLA Ops:
  1.3 56.0 %distill.1 = (f32[12,768]{1,0:T(8,128)S(1)}, f32[16,768]{1,0:T(8,128)S(1)}, f32[1,128]{1,0:T(1,128)S(1)}) custom-call(bf16[128,768]{1,0:T(8,128)(2,1)} %x_hbm.1, bf16[768,768]{1,0:T(8,128)(2,1)} %w_hbm.1, bf16[16,768]{1,0:T(8,128)(2,1)} %ts_hbm.1, bf16[128,1152]{1,0:T(8,128)(2,1)} %xt_hbm.1, bf16[16,1152]{1,0:T(8,128)(2,1)} %tt_hbm.1, f32[2]{0:T(128)} %scales_hbm.1, ...), custom_call_target="tpu_custom_call" | custom-call | tf_op jit(solution)/shard_map/distill/pallas_call | solution.py:457
  57.3 0.6 %copy.14 = f32[12,768]{1,0:T(8,128)} copy(f32[12,768]{1,0:T(8,128)S(1)} %get-tuple-element.9) | data formatting | bytes 73728
  57.9 0.5 copy.16
  58.4 0.6 %copy.15 = f32[16,768]{1,0:T(8,128)} copy(f32[16,768]{1,0:T(8,128)S(1)} %get-tuple-element.10) | data formatting | bytes 98304
